TPU v7x, 32 devices: a whole 2x2x4 slice. The times are simulated.
32 devices in a mesh: leaf: 8 (over z, x), probe: 4 (over y, core).
Axes of the slice: x: 2, y: 2, z: 4, core: 2. Of those that a mesh axis runs over, the one named last changes fastest.
Arguments:
- covariates: float32 [8, 8192], P(None, 'leaf'), may hold values from -6 to 6
- targets: float32 [8192], P('leaf'), may hold values from -18 to 18
- noise_var: float32 [8192], P('leaf'), may hold values from 0.5 to 2
- lengths: float32 [8], replicated, may hold values from 0.7 to 1.5
- frequencies: float32 [7, 8, 128], replicated, may hold values from -6 to 6
- phases: float32 [7, 128], replicated, may hold values from -3.140625 to 3.140625
- tree_order: int32 [8192], P('leaf'), may hold values from 0 to 8191, each once
- probe_seeds: int32 [64], P('probe'), may hold values from 0 to 16777215
Outputs:
- target_solve: float32 [8192], P('leaf')
- probe_solves: float32 [64, 8192], P('probe', 'leaf')
- noise_grad: float32 [8192], P('leaf')
Inputs may be any that keep to these rules, and one draw needn't show every extreme that they name: `tree_order`: each value 0 to 8191 appears exactly once.
All inputs are finite; a program needn't handle non-finite values.
Results may differ from a plain program's by a relative error of at most 0.00021.
Values sent between devices are 32-bit elements; how exact they have to be, the bound alone decides.
No kernel may reach another device: no remote copies, remote signals or barrier semaphores. Data moves between devices by JAX's collectives and lax.ppermute only.
A program may use at most 128 MiB of HBM per device.

v0:
```python
import jax
import jax.numpy as jnp
from jax import lax
from jax.sharding import PartitionSpec as P

PROBES = 64


highest = lax.Precision.HIGHEST
hash_first = 747796405
hash_second = -1403630843
hash_third = -2073254261


def partner_2(block, axis, apart):
    count = lax.axis_size(axis)
    route = []
    for low in range(count):
        high = low | 1 << apart
        if high != low and high < count:
            route += [(low, high), (high, low)]
    return lax.ppermute(block, axis, route)


def rademacher(seeds, positions):
    mixed = seeds[:, None] * jnp.int32(hash_first) + positions[None, :] * jnp.int32(hash_second)
    mixed = jnp.bitwise_xor(mixed, lax.shift_right_logical(mixed, jnp.full_like(mixed, 15)))
    mixed = mixed * jnp.int32(hash_third)
    mixed = jnp.bitwise_xor(mixed, lax.shift_right_logical(mixed, jnp.full_like(mixed, 13)))
    parity = jnp.bitwise_and(
        lax.shift_right_logical(mixed, jnp.full_like(mixed, 11)), jnp.full_like(mixed, 1)
    )
    return (2 * parity - 1).astype(jnp.float32)


def features(coords, omega, phase):
    angle = (
        jnp.dot(omega.T, coords, precision=highest, preferred_element_type=jnp.float32)
        + phase[:, None]
    )
    return jnp.sqrt(2.0 / omega.shape[1]) * jnp.cos(angle)


def leaf_matrix(coords, point_noise, lengths):
    scaled = coords / lengths[:, None]
    squared = jnp.sum(scaled * scaled, axis=0)
    cross = jnp.dot(scaled.T, scaled, precision=highest, preferred_element_type=jnp.float32)
    return jnp.exp(-0.5 * (squared[:, None] + squared[None, :] - 2.0 * cross)) + jnp.diag(
        point_noise
    )


def node_sum(gram_block, projected, height):
    for bit_number in range(height):
        partner = partner_2((gram_block, projected), "leaf", bit_number)
        gram_block = gram_block + partner[0]
        projected = projected + partner[1]
    return (gram_block, projected)


def shards(covariates, targets, noise_var, lengths, frequencies, phases, tree_order, probe_seeds):
    leaf_count = lax.axis_size("leaf")
    leaf_index = lax.axis_index("leaf")
    leaf_width = tree_order.shape[0]
    rank_width = phases.shape[1]
    feature_count = covariates.shape[0]
    levels = leaf_count.bit_length() - 1
    packed = jnp.concatenate([covariates, targets[None, :], noise_var[None, :]], axis=0)
    gathered = lax.all_gather(packed, "leaf", axis=1, tiled=True)
    local_data = jnp.take(gathered, tree_order, axis=1)
    coords = local_data[:feature_count]
    point_targets = local_data[feature_count]
    point_noise = local_data[feature_count + 1]
    positions = leaf_index * leaf_width + jnp.arange(leaf_width, dtype=jnp.int32)
    probe_signs = rademacher(probe_seeds, positions)
    right_sides = jnp.concatenate([point_targets[None, :], probe_signs], axis=0)
    heights = jnp.arange(1, levels + 1, dtype=jnp.int32)
    nodes = jnp.right_shift(leaf_count + leaf_index, heights)
    omega = frequencies[nodes - 1] / lengths[None, :, None]
    bases = [features(coords, omega[level], phases[nodes[level] - 1]) for level in range(levels)]
    factor = jnp.linalg.cholesky(leaf_matrix(coords, point_noise, lengths))
    columns = jnp.concatenate(bases + [right_sides], axis=0)
    solved = jax.scipy.linalg.cho_solve((factor, True), columns.T).T
    identity = jnp.eye(rank_width, dtype=jnp.float32)
    for height in range(1, levels + 1):
        basis_block = solved[:rank_width]
        remainder = solved[rank_width:]
        basis_rows = bases[height - 1]
        gram_block = jnp.dot(
            basis_block, basis_rows.T, precision=highest, preferred_element_type=jnp.float32
        )
        projected = jnp.dot(
            remainder, basis_rows.T, precision=highest, preferred_element_type=jnp.float32
        )
        gram_block, projected = node_sum(gram_block, projected, height)
        capacitance = identity + 0.5 * (gram_block + gram_block.T)
        factors = jnp.linalg.cholesky(capacitance)
        coefficients = jax.scipy.linalg.cho_solve((factors, True), projected.T)
        solved = remainder - jnp.dot(
            coefficients.T, basis_block, precision=highest, preferred_element_type=jnp.float32
        )
    target_solve = solved[0]
    probe_solves = solved[1:]
    local_terms = jnp.sum(probe_signs * probe_solves, axis=0)
    estimate = lax.psum(local_terms, "probe") / PROBES
    noise_grad = 0.5 * target_solve * target_solve - 0.5 * estimate
    return (target_solve, probe_solves, noise_grad)


def solution(mesh):
    in_specs = (P(None, "leaf"), P("leaf"), P("leaf"), P(), P(), P(), P("leaf"), P("probe"))
    out_specs = (P("leaf"), P("probe", "leaf"), P("leaf"))
    return jax.shard_map(shards, mesh=mesh, in_specs=in_specs, out_specs=out_specs, check_vma=False)
```

profile of v0, /device:TPU:0, one launch (start us, length us, event | category | flops | bytes accessed | tf_op | source)
XLA Modules:
  0.0 588.1 jit_solution(15880904877926455697)
XLA Ops:
  7.6 85.9 %all_gather.3 = f32[10,8192]{0,1:T(8,128)} all-gather(f32[10,1024]{0,1:T(8,128)S(1)} %copy.53), channel_id=1, replica_groups=mesh['leaf'=8,'probe'=4] {'leaf'}, dimensions={1}, use_global_device_ids=true | all-gather | bytes 368640 | tf_op jit(solution)/shard_map/all_gather | solution.py:69
  93.5 5.0 gather_fusion
  98.8 6.9 %multiply_subtract_fusion = (f32[1024,1024]{0,1:T(8,128)}, f32[1024,1024]{0,1:T(8,128)}, f32[1024,1024]{0,1:T(8,128)}) fusion(f32[1024]{0:T(1024)S(1)} %multiply_reduce_fusion.1, f32[10,1024]{1,0:T(8,128)S(1)} %select_bitcast_fusion, f32[8]{0:T(128)S(1)} %copy-done.6), kind=kOutput, calls=%fused_computation.14 | convolution fusion | flops 103817216 | bytes 12624384 | tf_op jit(solution)/shard_map/dot_general | solution.py:47
  105.7 5.3 copy.56
  111.0 5.4 copy.57
  116.4 6.3 %fusion.4 = f32[1024,1024]{1,0:T(8,128)S(1)} fusion(f32[1024,1024]{1,0:T(8,128)} %copy.57, f32[1024,1024]{1,0:T(8,128)} %copy.56, f32[1024,1024]{0,1:T(8,128)} %get-tuple-element.73, f32[1024]{0:T(1024)S(1)} %bitcast.240), kind=kLoop, calls=%fused_computation.10 | loop fusion | flops 12582912 | bytes 16781312 | tf_op jit(solution)/shard_map/jit(cholesky)/div | solution.py:81
  124.6 11.7 %cholesky.254 = f32[128,128]{1,0:T(8,128)S(1)} custom-call(f32[128,128]{1,0:T(8,128)S(1)} %cholesky.703), custom_call_target="Cholesky" | custom-call | tf_op jit(solution)/shard_map/jit(cholesky)/cholesky | solution.py:81
  136.4 9.8 %custom-call.89 = f32[1,128,128]{1,2,0:T(8,128)S(1)} custom-call(f32[1,128,128]{2,1,0:T(8,128)S(1)} %get-tuple-element.62), custom_call_target="InvertDiagBlocksLowerTriangular" | custom-call | tf_op jit(solution)/shard_map/jit(cholesky)/cholesky | solution.py:81
  146.2 2.5 cholesky.284
  148.7 2.4 constant_dynamic-update-slice_fusion.48
  152.6 11.7 %cholesky.277 = f32[128,128]{1,0:T(8,128)S(1)} custom-call(f32[128,128]{1,0:T(8,128)S(1)} %cholesky.707), custom_call_target="Cholesky" | custom-call | tf_op jit(solution)/shard_map/jit(cholesky)/cholesky | solution.py:81
  165.0 10.2 %custom-call.90 = f32[1,128,128]{1,2,0:T(8,128)S(1)} custom-call(f32[1,128,128]{2,1,0:T(8,128)S(1)} %get-tuple-element.59), custom_call_target="InvertDiagBlocksLowerTriangular" | custom-call | tf_op jit(solution)/shard_map/jit(cholesky)/cholesky | solution.py:81
  178.6 11.7 %cholesky.529 = f32[128,128]{1,0:T(8,128)S(1)} custom-call(f32[128,128]{1,0:T(8,128)S(1)} %cholesky.712), custom_call_target="Cholesky" | custom-call | tf_op jit(solution)/shard_map/jit(cholesky)/cholesky | solution.py:81
  191.5 9.8 %custom-call.91 = f32[1,128,128]{1,2,0:T(8,128)S(1)} custom-call(f32[1,128,128]{2,1,0:T(8,128)S(1)} %get-tuple-element.56), custom_call_target="InvertDiagBlocksLowerTriangular" | custom-call | tf_op jit(solution)/shard_map/jit(cholesky)/cholesky | solution.py:81
  202.5 2.4 convolution_subtract_fusion.4
  204.9 11.9 %cholesky.548 = f32[128,128]{1,0:T(8,128)S(1)} custom-call(f32[128,128]{1,0:T(8,128)S(1)} %cholesky.717), custom_call_target="Cholesky" | custom-call | tf_op jit(solution)/shard_map/jit(cholesky)/cholesky | solution.py:81
  218.1 9.8 %custom-call.92 = f32[1,128,128]{1,2,0:T(8,128)S(1)} custom-call(f32[1,128,128]{2,1,0:T(8,128)S(1)} %get-tuple-element.53), custom_call_target="InvertDiagBlocksLowerTriangular" | custom-call | tf_op jit(solution)/shard_map/jit(cholesky)/cholesky | solution.py:81
  229.0 2.3 convolution_subtract_fusion.5
  231.3 11.7 %cholesky.567 = f32[128,128]{1,0:T(8,128)S(1)} custom-call(f32[128,128]{1,0:T(8,128)S(1)} %cholesky.722), custom_call_target="Cholesky" | custom-call | tf_op jit(solution)/shard_map/jit(cholesky)/cholesky | solution.py:81
  244.3 9.8 %custom-call.93 = f32[1,128,128]{1,2,0:T(8,128)S(1)} custom-call(f32[1,128,128]{2,1,0:T(8,128)S(1)} %get-tuple-element.50), custom_call_target="InvertDiagBlocksLowerTriangular" | custom-call | tf_op jit(solution)/shard_map/jit(cholesky)/cholesky | solution.py:81
  255.2 2.7 convolution_subtract_fusion.20
  257.9 11.7 %cholesky.587 = f32[128,128]{1,0:T(8,128)S(1)} custom-call(f32[128,128]{1,0:T(8,128)S(1)} %cholesky.727), custom_call_target="Cholesky" | custom-call | tf_op jit(solution)/shard_map/jit(cholesky)/cholesky | solution.py:81
  270.9 9.8 %custom-call.94 = f32[1,128,128]{1,2,0:T(8,128)S(1)} custom-call(f32[1,128,128]{2,1,0:T(8,128)S(1)} %get-tuple-element.47), custom_call_target="InvertDiagBlocksLowerTriangular" | custom-call | tf_op jit(solution)/shard_map/jit(cholesky)/cholesky | solution.py:81
  283.7 11.7 %cholesky.607 = f32[128,128]{1,0:T(8,128)S(1)} custom-call(f32[128,128]{1,0:T(8,128)S(1)} %cholesky.732), custom_call_target="Cholesky" | custom-call | tf_op jit(solution)/shard_map/jit(cholesky)/cholesky | solution.py:81
  296.7 10.0 %custom-call.95 = f32[1,128,128]{1,2,0:T(8,128)S(1)} custom-call(f32[1,128,128]{2,1,0:T(8,128)S(1)} %get-tuple-element.44), custom_call_target="InvertDiagBlocksLowerTriangular" | custom-call | tf_op jit(solution)/shard_map/jit(cholesky)/cholesky | solution.py:81
  309.2 11.7 %cholesky.625 = f32[128,128]{1,0:T(8,128)S(1)} custom-call(f32[128,128]{1,0:T(8,128)S(1)} %convolution_subtract_fusion.23), custom_call_target="Cholesky" | custom-call | tf_op jit(solution)/shard_map/jit(cholesky)/cholesky | solution.py:81
  327.8 4.8 select_select_fusion
  332.6 22.8 %while.1 = (s32[]{:T(128)}, f32[1024,1024]{1,0:T(8,128)}, s32[8,2]{0,1:T(2,128)S(1)}, f32[8,128,128]{2,1,0:T(8,128)S(1)}, s32[]{:T(128)}) while((s32[]{:T(128)}, f32[1024,1024]{1,0:T(8,128)}, s32[8,2]{0,1:T(2,128)S(1)}, f32[8,128,128]{2,1,0:T(8,128)S(1)}, s32[]{:T(128)}) %tuple.69), condition=%wide.while_cond, body=%wide.while_body.sunk | while | flops 2 | bytes 131181 | solution.py:83
  333.2 2.2 bitcast_dynamic-update-slice_fusion.2
  341.8 2.2 bitcast_dynamic-update-slice_fusion.2
  347.6 2.2 bitcast_dynamic-update-slice_fusion.2
  355.5 79.2 %custom-call.96 = f32[8,128,128]{1,2,0:T(8,128)} custom-call(f32[8,128,128]{2,1,0:T(8,128)S(1)} %get-tuple-element.11), custom_call_target="InvertDiagBlocksLowerTriangular" | custom-call | tf_op jit(solution)/shard_map/jit(_cho_solve)/triangular_solve | solution.py:83
  436.1 2.3 fusion.8
  438.4 2.3 fusion.9
  440.7 2.3 fusion.10
  476.1 11.9 %cholesky.672 = f32[128,128]{1,0:T(8,128)S(1)} custom-call(f32[128,128]{1,0:T(8,128)S(1)} %copy.62), custom_call_target="Cholesky" | custom-call | tf_op jit(solution)/shard_map/jit(cholesky)/cholesky | solution.py:97
  489.3 9.8 %custom-call.97 = f32[1,128,128]{1,2,0:T(8,128)S(1)} custom-call(f32[1,128,128]{2,1,0:T(8,128)S(1)} %fusion.92), custom_call_target="InvertDiagBlocksLowerTriangular" | custom-call | tf_op jit(solution)/shard_map/jit(_cho_solve)/triangular_solve | solution.py:98
  499.9 2.5 convolution_subtract_fusion
  512.1 12.0 %cholesky.683 = f32[128,128]{1,0:T(8,128)S(1)} custom-call(f32[128,128]{1,0:T(8,128)S(1)} %copy.67), custom_call_target="Cholesky" | custom-call | tf_op jit(solution)/shard_map/jit(cholesky)/cholesky | solution.py:97
  525.4 9.8 %custom-call.98 = f32[1,128,128]{1,2,0:T(8,128)S(1)} custom-call(f32[1,128,128]{2,1,0:T(8,128)S(1)} %fusion.93), custom_call_target="InvertDiagBlocksLowerTriangular" | custom-call | tf_op jit(solution)/shard_map/jit(_cho_solve)/triangular_solve | solution.py:98
  537.1 4.3 collective-permute-done.6
  541.4 4.4 collective-permute-done.7
  547.7 2.6 collective-permute-done.9
  551.2 2.8 collective-permute-done.10
  554.0 2.8 collective-permute-start.11
  557.1 11.7 %cholesky.694 = f32[128,128]{1,0:T(8,128)S(1)} custom-call(f32[128,128]{1,0:T(8,128)S(1)} %copy.72), custom_call_target="Cholesky" | custom-call | tf_op jit(solution)/shard_map/jit(cholesky)/cholesky | solution.py:97
  570.2 9.8 %custom-call.99 = f32[1,128,128]{1,2,0:T(8,128)S(1)} custom-call(f32[1,128,128]{2,1,0:T(8,128)S(1)} %fusion.94), custom_call_target="InvertDiagBlocksLowerTriangular" | custom-call | tf_op jit(solution)/shard_map/jit(_cho_solve)/triangular_solve | solution.py:98
  581.4 5.6 psum.7
  (212 shorter events, 99.5 us)
Async XLA Ops:
  0.6 434.1 %copy-start = (f32[7,8,128]{2,1,0:T(8,128)S(1)}, f32[7,8,128]{2,1,0:T(8,128)}, u32[]{:S(2)}) copy-start(f32[7,8,128]{2,1,0:T(8,128)} %param.13) | copy-start | bytes 86020
  0.6 98.1 %copy-start.6 = (f32[8]{0:T(128)S(1)}, f32[8]{0:T(128)}, u32[]{:S(2)}) copy-start(f32[8]{0:T(128)} %param.12) | copy-start | bytes 100
  122.7 1.9 copy-start.2
  327.8 115.2 %copy-start.7 = (s32[16]{0:T(128)S(1)}, s32[16]{0:T(128)}, u32[]{:S(2)}) copy-start(s32[16]{0:T(128)} %param.16) | copy-start | bytes 196
  444.1 6.9 %copy-start.1 = (f32[1024,1024]{1,0:T(8,128)S(1)}, f32[1024,1024]{1,0:T(8,128)}, u32[]{:S(2)}) copy-start(f32[1024,1024]{1,0:T(8,128)} %get-tuple-element.136) | copy-start | bytes 12582916
  444.1 7.7 %copy-start.4 = (f32[8,128,128]{1,2,0:T(8,128)S(1)}, f32[8,128,128]{1,2,0:T(8,128)}, u32[]{:S(2)}) copy-start(f32[8,128,128]{1,2,0:T(8,128)} %custom-call.96) | copy-start | bytes 1572868
  470.1 1.7 copy-start.3
  470.7 5.0 collective-permute-start
  471.8 27.3 %collective-permute-start.1 = (f32[273,128]{1,0:T(8,128)S(1)}, f32[273,128]{1,0:T(8,128)S(1)}, u32[]{:S(2)}, u32[]{:S(2)}) collective-permute-start(f32[273,128]{1,0:T(8,128)S(1)} %fusion.11), channel_id=1, source_target_pairs={{0,4},{4,0},{8,12},{12,8},{16,20},{20,16},{24,28},{28,24},{1,5},{5... | collective-permute-start | bytes 419336 | tf_op jit(solution)/shard_map/ppermute | solution.py:22
  503.0 4.3 collective-permute-start.2
  503.8 4.5 collective-permute-start.4
  507.4 4.3 collective-permute-start.3
  508.3 26.9 %collective-permute-start.5 = (f32[145,128]{1,0:T(8,128)S(1)}, f32[145,128]{1,0:T(8,128)S(1)}, u32[]{:S(2)}, u32[]{:S(2)}) collective-permute-start(f32[145,128]{1,0:T(8,128)S(1)} %add.347), channel_id=1, source_target_pairs={{0,8},{8,0},{4,12},{12,4},{16,24},{24,16},{20,28},{28,20},{1,9},{9... | collective-permute-start | bytes 222728 | tf_op jit(solution)/shard_map/ppermute | solution.py:22
  537.0 4.3 collective-permute-start.6
  541.4 4.5 collective-permute-start.7
  545.8 10.9 %collective-permute-start.8 = (f32[128,128]{0,1:T(8,128)S(1)}, f32[128,128]{0,1:T(8,128)S(1)}, u32[]{:S(2)}, u32[]{:S(2)}) collective-permute-start(f32[128,128]{0,1:T(8,128)S(1)} %add.350), channel_id=1, source_target_pairs={{0,16},{16,0},{4,20},{20,4},{8,24},{24,8},{12,28},{28,12},{1,17},{... | collective-permute-start | bytes 196616 | tf_op jit(solution)/shard_map/ppermute | solution.py:22
  546.6 3.7 collective-permute-start.9
  550.3 3.7 collective-permute-start.10
  554.0 26.0 %collective-permute-start.11 = (f32[17,128]{1,0:T(8,128)S(1)}, f32[17,128]{1,0:T(8,128)S(1)}, u32[]{:S(2)}, u32[]{:S(2)}) collective-permute-start(f32[17,128]{1,0:T(8,128)S(1)} %add.355), channel_id=1, source_target_pairs={{0,16},{16,0},{4,20},{20,4},{8,24},{24,8},{12,28},{28,12},{1,17},{... | collective-permute-start | bytes 26120 | tf_op jit(solution)/shard_map/ppermute | solution.py:22
  581.4 6.3 %copy-start.5 = (f32[1,1024]{1,0:T(1,128)}, f32[1,1024]{1,0:T(1,128)S(1)}, u32[]{:S(2)}) copy-start(f32[1,1024]{1,0:T(1,128)S(1)} %slice.450) | copy-start | bytes 12292
where the time goes:
time: 593 us; the launch traced here: 588 us
  other arithmetic  335 us (56%)
  blocking collectives  91.5 us (15%)
  matrix products  71.7 us (12%)
  local copies, waits for them, and re-layouts  47.4 us (8%)
  waiting for transfers between devices  20.2 us (3%)
  starting transfers between devices  10.9 us (2%)
  between operations  10.9 us (2%)
    another operation x30, other arithmetic, shards(): factor = jnp.linalg.cholesky(leaf_matrix(coords, point_noise, lengths))  172 us
    all_gather x1, blocking collectives, shards(): gathered = lax.all_gather(packed, 'leaf', axis=1, tiled=True)  85.9 us
    another operation x3, other arithmetic, shards(): solved = jax.scipy.linalg.cho_solve((factor, True), columns.T).T  84 us
    another operation x9, other arithmetic, shards(): factors = jnp.linalg.cholesky(capacitance)  37.6 us
    another operation x6, other arithmetic, shards(): coefficients = jax.scipy.linalg.cho_solve((factors, True), projected.T)  31.4 us
    another operation x30, matrix products, shards(): solved = jax.scipy.linalg.cho_solve((factor, True), columns.T).T  25.2 us
    another operation x14, matrix products, shards(): factor = jnp.linalg.cholesky(leaf_matrix(coords, point_noise, lengths))  23.6 us
    another operation x24, local copies, waits for them, and re-layouts  22.7 us
  transfers between devices with their start and end apart: 12, of which 8 were waited for; matrix products, arithmetic and copies ran while one was open for 12% of the time, Pallas kernels for 0%

commit v1 on v0

v1 whole, which is shorter than its diff:
```python
import functools
import math

import jax
import jax.numpy as jnp
from jax import lax
from jax.experimental import pallas as pl
from jax.experimental.pallas import tpu as pltpu
from jax.sharding import PartitionSpec as P

PROBES = 64
BLOCK = 256
SETTLED = 1.001

f32 = jnp.float32
bf16 = jnp.bfloat16
highest = lax.Precision.HIGHEST
hash_first = 747796405
hash_second = -1403630843
hash_third = -2073254261
VMEM_BYTES = 40 * 1024 * 1024


def partner_of(block, axis, apart):
    count = lax.axis_size(axis)
    return lax.ppermute(block, axis, [(i, i ^ (1 << apart)) for i in range(count)])


def halves(x):
    high = x.astype(bf16)
    return high, (x - high.astype(f32)).astype(bf16)


def thirds(x):
    high = x.astype(bf16)
    rest = x - high.astype(f32)
    middle = rest.astype(bf16)
    return high, middle, (rest - middle.astype(f32)).astype(bf16)


NN = (((1,), (0,)), ((), ()))
NT = (((1,), (1,)), ((), ()))
TN = (((0,), (0,)), ((), ()))


def dot_one(a, b, dims=NN):
    return lax.dot_general(a, b, dims, preferred_element_type=f32)


def dot_three(a, b, dims=NN):
    a_high, a_low = halves(a)
    b_high, b_low = halves(b)
    return dot_one(a_high, b_high, dims) + (dot_one(a_high, b_low, dims) + dot_one(a_low, b_high, dims))


def dot_full(a, b, dims=NN):
    return lax.dot_general(a, b, dims, precision=highest, preferred_element_type=f32)


def unit(size):
    rows = lax.broadcasted_iota(jnp.int32, (size, size), 0)
    columns = lax.broadcasted_iota(jnp.int32, (size, size), 1)
    return rows == columns


def gain(ratio):
    reach = (ratio - 1.0) / (ratio + 1.0)
    return 2.0 / (2.0 - reach * reach)


def tighter(ratio):
    return (ratio + 1.0) * (ratio + 1.0) / (4.0 * ratio)


def inverse(matrix, low, residual, approx):
    size = matrix.shape[0]
    same = unit(size)
    high = jnp.max(jnp.sum(jnp.abs(matrix), axis=0, keepdims=True)) * 1.0001
    low = jnp.minimum(low, high) * 0.9999
    scale = 2.0 / (low + high)
    ratio = high / low
    c = gain(ratio)
    first = jnp.where(same, 1.0, 0.0) - scale * matrix
    residual[...] = c * dot_three(first, first) - jnp.where(same, c - 1.0, 0.0)
    approx[...] = (c * scale) * (first + jnp.where(same, 1.0, 0.0))

    def more(ratio):
        return tighter(ratio) > SETTLED

    def double(ratio):
        c = gain(ratio)
        e = residual[...]
        x = approx[...]
        squared = dot_three(e, e)
        moved = dot_three(x, e)
        residual[...] = c * squared - jnp.where(same, c - 1.0, 0.0)
        approx[...] = c * (x + moved)
        return tighter(ratio)

    ratio = lax.while_loop(more, double, tighter(ratio))
    x = approx[...]
    x = gain(ratio) * (x + dot_three(x, residual[...]))
    left = jnp.where(same, 1.0, 0.0) - dot_full(x, matrix)
    return x + dot_three(left, x)


def cosine(x):
    turns = jnp.floor(x * (1.0 / math.pi) + 0.5)
    r = x - turns * 3.140625
    r = r - turns * 9.67502593994140625e-4
    r = r - turns * 1.509957990978376e-7
    odd = jnp.bitwise_and(turns.astype(jnp.int32), 1)
    s = r * r
    value = 1.0 / 479001600.0
    for term in (-1.0 / 3628800.0, 1.0 / 40320.0, -1.0 / 720.0, 1.0 / 24.0, -0.5, 1.0):
        value = value * s + term
    return jnp.where(odd == 1, -value, value)


def logical_right(x, by):
    return lax.shift_right_logical(x, jnp.full_like(x, by))


def signs_of(seeds, positions):
    mixed = seeds * jnp.int32(hash_first) + positions * jnp.int32(hash_second)
    mixed = jnp.bitwise_xor(mixed, logical_right(mixed, 15))
    mixed = mixed * jnp.int32(hash_third)
    mixed = jnp.bitwise_xor(mixed, logical_right(mixed, 13))
    parity = jnp.bitwise_and(logical_right(mixed, 11), jnp.full_like(mixed, 1))
    return (2 * parity - 1).astype(f32)


def leaf_kernel(levels, place_ref, data_ref, length_ref, frequency_ref, phase_ref, seed_ref,
                lower_ref, aug_ref, gram_ref, matrix, residual, approx):
    width = data_ref.shape[1]
    rank = frequency_ref.shape[2]
    covs = length_ref.shape[0]
    probes = seed_ref.shape[0]
    blocks = width // BLOCK
    top = width + levels * rank
    u = data_ref[0:covs, :] / length_ref[...]
    s = -0.5 * jnp.sum(u * u, axis=0, keepdims=True)
    u_parts = [p.astype(f32) for p in thirds(u)]
    h, m, l = u_parts
    row = lax.broadcasted_iota(jnp.int32, (8, width), 0)
    ones = jnp.where(row < 3, 1.0, 0.0)
    for level in range(levels):
        node = jnp.right_shift(place_ref[1], level + 1) - 1
        fh, fm, fl = [p.astype(f32) for p in thirds(frequency_ref[node])]
        ph, pm, p_low = [p.astype(f32) for p in thirds(phase_ref[pl.ds(node, 1), :])]
        at_row = lax.broadcasted_iota(jnp.int32, (8, rank), 0)
        phases = jnp.where(at_row == 0, ph, jnp.where(at_row == 1, pm, jnp.where(at_row == 2, p_low, 0.0)))
        left = jnp.concatenate([fh, fh, fm, fm, fh, fl, phases, jnp.zeros_like(phases)], axis=0).astype(bf16)
        right = jnp.concatenate([h, m, h, m, l, h, ones, ones], axis=0).astype(bf16)
        angle = dot_one(left, right, TN)
        matrix[width + level * rank:width + (level + 1) * rank, :] = math.sqrt(2.0 / rank) * cosine(angle)
    positions = place_ref[0] + lax.broadcasted_iota(jnp.int32, (probes, width), 1)
    matrix[top:top + probes, :] = signs_of(seed_ref[...], positions)
    matrix[top + probes:, :] = jnp.concatenate(
        [data_ref[covs:covs + 1, :], jnp.zeros((matrix.shape[0] - top - probes - 1, width), f32)], axis=0)
    s_parts = [p.astype(f32) for p in thirds(s)]
    s_rows = jnp.where(row == 0, s_parts[0], jnp.where(row == 1, s_parts[1], jnp.where(row == 2, s_parts[2], 0.0)))
    left = jnp.concatenate([h, h, m, m, h, l, s_rows, ones], axis=0).astype(bf16)
    right = jnp.concatenate([h, m, h, m, l, h, ones, s_rows], axis=0).astype(bf16)
    noise = data_ref[covs + 1:covs + 2, :]
    same = unit(BLOCK)
    spans = [slice(k * BLOCK, (k + 1) * BLOCK) for k in range(blocks)]
    for i in range(blocks):
        for j in range(i + 1):
            part = jnp.exp(dot_one(left[:, spans[i]], right[:, spans[j]], TN))
            if i == j:
                part = part + jnp.where(same, noise[:, spans[i]], 0.0)
            matrix[spans[i], spans[j]] = part
    rows = matrix.shape[0]
    for k in range(blocks):
        block_inverse = inverse(matrix[spans[k], spans[k]], jnp.min(noise[:, spans[k]]), residual, approx)
        below = (k + 1) * BLOCK
        column = matrix[below:, spans[k]]
        weights = dot_full(column, block_inverse)
        for j in range(k + 1, blocks):
            start = j * BLOCK
            matrix[start:, spans[j]] = matrix[start:, spans[j]] - dot_full(
                weights[start - below:], column[start - below:start - below + BLOCK], NT)
        at = 0
        for level in range(levels):
            start = width + level * rank
            part = dot_full(weights[start - below:], column[start - below:start - below + rank], NT)
            count = rows - start
            if k == 0:
                gram_ref[at:at + count, :] = part
            else:
                gram_ref[at:at + count, :] += part
            at += count
        aug_ref[:, spans[k]] = weights[width - below:]
        if k + 1 < blocks:
            lower_ref[k * BLOCK:, spans[k]] = weights[:width - below]


def eliminate(own, other, rank, residual, approx):
    total = own + other
    capacitance = total[:rank] + jnp.where(unit(rank), 1.0, 0.0)
    return total, dot_full(total[rank:], inverse(capacitance, jnp.float32(1.0), residual, approx))


def height_kernel(left, tail, own_ref, other_ref, coefficient_ref, rest_ref, residual, approx):
    rank = own_ref.shape[1]
    count = left * rank + tail
    total, coefficients = eliminate(own_ref[:count, :], other_ref[:count, :], rank, residual, approx)
    coefficient_ref[...] = coefficients
    at, to = count, 0
    for level in range(1, left):
        size = (left - level) * rank + tail
        start = (level - 1) * rank
        rest_ref[to:to + size, :] = own_ref[at:at + size, :] + other_ref[at:at + size, :] - dot_full(
            coefficients[start:], total[level * rank:(level + 1) * rank], NT)
        at += size
        to += size


def final_kernel(levels, probes, tail, *refs):
    own_ref, other_ref = refs[:2]
    coefficient_refs = refs[2:2 + levels - 1]
    lower_ref, aug_ref, seed_ref, first_ref = refs[1 + levels:5 + levels]
    target_ref, solve_ref, terms_ref, residual, approx = refs[5 + levels:]
    rank = own_ref.shape[1]
    width = aug_ref.shape[1]
    blocks = width // BLOCK
    _, last = eliminate(own_ref[...], other_ref[...], rank, residual, approx)
    combined = [None] * levels
    combined[levels - 1] = last
    for level in range(levels - 2, -1, -1):
        below = coefficient_refs[level]
        value = below[(levels - 1 - level) * rank:, :]
        for later in range(level + 1, levels):
            start = (later - level - 1) * rank
            value = value - dot_full(combined[later], below[start:start + rank, :])
        combined[level] = value
    value = aug_ref[levels * rank:, :] - dot_full(jnp.concatenate(combined, axis=1), aug_ref[:levels * rank, :])
    parts = [value[:, k * BLOCK:(k + 1) * BLOCK] for k in range(blocks)]
    for k in range(blocks - 1, 0, -1):
        moved = dot_full(parts[k], lower_ref[(k - 1) * BLOCK:k * BLOCK, :k * BLOCK])
        for j in range(k):
            parts[j] = parts[j] - moved[:, j * BLOCK:(j + 1) * BLOCK]
    solved = jnp.concatenate(parts, axis=1)
    positions = first_ref[0] + lax.broadcasted_iota(jnp.int32, (probes, width), 1)
    solve_ref[...] = solved[:probes]
    target_ref[...] = solved[probes:probes + 1]
    terms_ref[...] = jnp.sum(signs_of(seed_ref[...], positions) * solved[:probes], axis=0, keepdims=True)


def whole(count=1):
    return [pl.BlockSpec(memory_space=pltpu.VMEM)] * count


def scalars():
    return pl.BlockSpec(memory_space=pltpu.SMEM)


def shards(covariates, targets, noise_var, lengths, frequencies, phases, tree_order, probe_seeds):
    leaf_count = lax.axis_size("leaf")
    leaf_index = lax.axis_index("leaf")
    width = tree_order.shape[0]
    rank = phases.shape[1]
    probes = probe_seeds.shape[0]
    levels = leaf_count.bit_length() - 1
    tail = -(-(probes + 1) // 8) * 8
    packed = jnp.concatenate([covariates, targets[None, :], noise_var[None, :]], axis=0)
    pieces = [packed]
    for k in range(1, leaf_count):
        pieces.append(lax.ppermute(packed, "leaf", [(i, (i + k) % leaf_count) for i in range(leaf_count)]))
    gathered = jnp.concatenate(pieces, axis=1)
    owner = jnp.right_shift(tree_order, width.bit_length() - 1)
    place = jnp.bitwise_and(leaf_index - owner, leaf_count - 1) * width + jnp.bitwise_and(tree_order, width - 1)
    data = jnp.take(gathered, place, axis=1)
    first = jnp.stack([leaf_index * width, leaf_count + leaf_index]).astype(jnp.int32)
    seeds = probe_seeds[:, None]
    sizes = [(levels - level) * rank + tail for level in range(levels)]
    params = pltpu.CompilerParams(vmem_limit_bytes=VMEM_BYTES)
    lower, aug, sums = pl.pallas_call(
        functools.partial(leaf_kernel, levels),
        out_shape=(
            jax.ShapeDtypeStruct((width - BLOCK, width - BLOCK), f32),
            jax.ShapeDtypeStruct((levels * rank + tail, width), f32),
            jax.ShapeDtypeStruct((sum(sizes), rank), f32),
        ),
        in_specs=[scalars()] + whole(5),
        out_specs=tuple(whole(3)),
        scratch_shapes=[
            pltpu.VMEM((width + levels * rank + tail, width), f32),
            pltpu.VMEM((BLOCK, BLOCK), f32),
            pltpu.VMEM((BLOCK, BLOCK), f32),
        ],
        compiler_params=params,
        name="leaf",
    )(first, data, lengths[:, None], frequencies, phases, seeds)
    small = [pltpu.VMEM((rank, rank), f32), pltpu.VMEM((rank, rank), f32)]
    coefficients = []
    for height in range(1, levels):
        left = levels - height + 1
        other = partner_of(sums, "leaf", height - 1)
        coefficient, sums = pl.pallas_call(
            functools.partial(height_kernel, left, tail),
            out_shape=(
                jax.ShapeDtypeStruct((sizes[height - 1] - rank, rank), f32),
                jax.ShapeDtypeStruct((sum(sizes[height:]), rank), f32),
            ),
            in_specs=whole(2),
            out_specs=tuple(whole(2)),
            scratch_shapes=small,
            compiler_params=params,
            name=f"height_{height}",
        )(sums, other)
        coefficients.append(coefficient)
    other = partner_of(sums, "leaf", levels - 1)
    target_solve, probe_solves, terms = pl.pallas_call(
        functools.partial(final_kernel, levels, probes, tail),
        out_shape=(
            jax.ShapeDtypeStruct((1, width), f32),
            jax.ShapeDtypeStruct((probes, width), f32),
            jax.ShapeDtypeStruct((1, width), f32),
        ),
        in_specs=whole(2 + levels - 1 + 3) + [scalars()],
        out_specs=tuple(whole(3)),
        scratch_shapes=small,
        compiler_params=params,
        name="final",
    )(sums, other, *coefficients, lower, aug, seeds, first)
    for bit in range(lax.axis_size("probe").bit_length() - 1):
        terms = terms + partner_of(terms, "probe", bit)
    target_solve = target_solve[0]
    noise_grad = 0.5 * target_solve * target_solve - 0.5 * (terms[0] / PROBES)
    return (target_solve, probe_solves, noise_grad)


def solution(mesh):
    in_specs = (P(None, "leaf"), P("leaf"), P("leaf"), P(), P(), P(), P("leaf"), P("probe"))
    out_specs = (P("leaf"), P("probe", "leaf"), P("leaf"))
    return jax.shard_map(shards, mesh=mesh, in_specs=in_specs, out_specs=out_specs, check_vma=False)
```

time: 593 us -> 99 us (0.17)
  other arithmetic: 335 us -> 3.6 us
  blocking collectives: 91.5 us -> 0 us
  matrix products: 71.7 us -> 0 us
  local copies, waits for them, and re-layouts: 47.4 us -> 9.34 us
  Pallas kernels: 0 us -> 36.6 us
  waiting for transfers between devices: 20.2 us -> 30.9 us
  between operations: 10.9 us -> 0.79 us
    another operation x48 -> x1, other arithmetic: 325 us -> 0.07 us  [shards(): jnp.stack([leaf_index * width, leaf_count + leaf_index]).astype(jnp.int32)]
    all_gather x1 -> x0, blocking collectives: 85.9 us -> none  [shards(): gathered = lax.all_gather(packed, 'leaf', axis=1, tiled=True)]
    another operation x50 -> x0, matrix products: 50.5 us -> none  [the longest x30 25.2 us: shards(): solved = jax.scipy.linalg.cho_solve((factor, True), columns.T).T]
    pallas_call x0 -> x4, Pallas kernels: none -> 36.6 us  [the longest x1 25.8 us: shards(): pl.pallas_call(functools.partial(leaf_kernel, levels), out_shape=(jax.Sha...]
    another operation x37 -> x0, local copies, waits for them, and re-layouts: 25.3 us -> none
    dot_general x13 -> x0, matrix products: 21.3 us -> none  [the longest x1 6.87 us: leaf_matrix(): jnp.dot(scaled.T, scaled, precision=highest, preferred_element_type=jnp.f...]
    ppermute x12, waiting for transfers between devices: 20.2 us -> 30.9 us  [the longest x5 17.9 us: partner_of(): lax.ppermute(block, axis, [(i, i ^ 1 << apart) for i in range(count)])]
    add x8 -> x0, local copies, waits for them, and re-layouts: 6.7 us -> none  [the longest x1 5.37 us: leaf_matrix(): squared[:, None] + squared[None, :] - 2.0 * cross]
  transfers between devices with their start and end apart: 12 -> 12, of which waited for: 8 -> 8; matrix products, arithmetic and copies ran while one was open for 12% -> 3% of each run, Pallas kernels for 0% -> 0%
where the time goes in v1:
time: 99 us; the launch traced here: 98 us
  Pallas kernels  36.6 us (37%)
  waiting for transfers between devices  30.9 us (31%)
  starting transfers between devices  16.8 us (17%)
  local copies, waits for them, and re-layouts  9.34 us (9%)
  other arithmetic  3.6 us (4%)
    pallas_call x1, Pallas kernels, shards(): pl.pallas_call(functools.partial(leaf_kernel, levels), out_shape=(jax.Sha...  25.8 us
    ppermute x5, waiting for transfers between devices, partner_of(): lax.ppermute(block, axis, [(i, i ^ 1 << apart) for i in range(count)])  17.9 us
    ppermute x7, waiting for transfers between devices, shards(): lax.ppermute(packed, 'leaf', [(i, (i + k) % leaf_count) for i in range(le...  12.9 us
    ppermute x7, starting transfers between devices, shards(): lax.ppermute(packed, 'leaf', [(i, (i + k) % leaf_count) for i in range(le...  10.4 us
    ppermute x5, starting transfers between devices, partner_of(): lax.ppermute(block, axis, [(i, i ^ 1 << apart) for i in range(count)])  6.42 us
    pallas_call x1, Pallas kernels, shards(): pl.pallas_call(functools.partial(final_kernel, levels, probes, tail), out...  5.6 us
    pallas_call x2, Pallas kernels, shards(): pl.pallas_call(functools.partial(height_kernel, left, tail), out_shape=(j...  5.2 us
    gather x2, local copies, waits for them, and re-layouts, shards(): data = jnp.take(gathered, place, axis=1)  5.18 us
  transfers between devices with their start and end apart: 12, of which 8 were waited for; matrix products, arithmetic and copies ran while one was open for 3% of the time, Pallas kernels for 0%

profile of v1, /device:TPU:0, one launch (start us, length us, event | category | flops | bytes accessed | tf_op | source)
XLA Modules:
  0.0 98.0 jit_solution(12258306687978795823)
XLA Ops:
  0.6 0.0 copy-start.1
  0.6 0.0 copy-start
  0.7 0.8 pad_maximum_fusion
  1.5 5.1 %collective-permute-start.5 = (f32[10,1024]{1,0:T(8,128)S(1)}, f32[10,1024]{1,0:T(8,128)S(1)}, u32[]{:S(2)}, u32[]{:S(2)}) collective-permute-start(f32[10,1024]{1,0:T(8,128)S(1)} %get-tuple-element.23), channel_id=1, source_target_pairs={{0,24},{4,28},{8,0},{12,4},{16,8},{20,12},{24,16},{28,20},{1,25},{... | collective-permute-start | bytes 122888 | tf_op jit(solution)/shard_map/ppermute | solution.py:270
  6.6 0.4 collective-permute-start.4
  6.9 3.5 %collective-permute-start.3 = (f32[10,1024]{1,0:T(8,128)S(1)}, f32[10,1024]{1,0:T(8,128)S(1)}, u32[]{:S(2)}, u32[]{:S(2)}) collective-permute-start(f32[10,1024]{1,0:T(8,128)S(1)} %get-tuple-element.23), channel_id=1, source_target_pairs={{0,16},{4,20},{8,24},{12,28},{16,0},{20,4},{24,8},{28,12},{1,17},{... | collective-permute-start | bytes 122888 | tf_op jit(solution)/shard_map/ppermute | solution.py:270
  10.4 0.0 collective-permute-start.2
  10.4 1.5 %collective-permute-start = (f32[10,1024]{1,0:T(8,128)S(1)}, f32[10,1024]{1,0:T(8,128)S(1)}, u32[]{:S(2)}, u32[]{:S(2)}) collective-permute-start(f32[10,1024]{1,0:T(8,128)S(1)} %get-tuple-element.23), channel_id=1, source_target_pairs={{0,4},{4,8},{8,12},{12,16},{16,20},{20,24},{24,28},{28,0},{1,5},{5... | collective-permute-start | bytes 122888 | tf_op jit(solution)/shard_map/ppermute | solution.py:270
  11.9 0.7 compare_and_fusion
  12.6 0.7 broadcast_clamp_fusion
  13.3 0.1 pad_add_fusion.place_ref.refs_7_
  13.4 0.7 copy.25.length_ref
  14.1 0.7 copy.26.seed_ref.refs_6_
  14.8 2.7 %collective-permute-done = f32[10,1024]{1,0:T(8,128)S(1)} collective-permute-done((f32[10,1024]{1,0:T(8,128)S(1)}, f32[10,1024]{1,0:T(8,128)S(1)}, u32[]{:S(2)}, u32[]{:S(2)}) %collective-permute-start) | collective-permute-done | bytes 40992 | tf_op jit(solution)/shard_map/ppermute | solution.py:270
  17.5 0.0 collective-permute-start.1
  17.5 6.1 %collective-permute-done.1 = f32[10,1024]{1,0:T(8,128)S(1)} collective-permute-done((f32[10,1024]{1,0:T(8,128)S(1)}, f32[10,1024]{1,0:T(8,128)S(1)}, u32[]{:S(2)}, u32[]{:S(2)}) %collective-permute-start.1) | collective-permute-done | bytes 40992 | tf_op jit(solution)/shard_map/ppermute | solution.py:270
  23.6 0.0 collective-permute-start.6
  23.6 0.0 collective-permute-done.2
  23.6 0.0 collective-permute-done.3
  23.7 0.0 collective-permute-done.4
  23.7 0.0 collective-permute-done.5
  23.7 4.2 %collective-permute-done.6 = f32[10,1024]{1,0:T(8,128)S(1)} collective-permute-done((f32[10,1024]{1,0:T(8,128)S(1)}, f32[10,1024]{1,0:T(8,128)S(1)}, u32[]{:S(2)}, u32[]{:S(2)}) %collective-permute-start.6) | collective-permute-done | bytes 40992 | tf_op jit(solution)/shard_map/ppermute | solution.py:270
  27.9 2.6 %copy.23 = f32[10,8192]{0,1:T(8,128)} copy(f32[10,8192]{1,0:T(8,128)S(1)} %constant_dynamic-update-slice_fusion) | data formatting | bytes 655360 | tf_op jit(solution)/shard_map/concatenate | solution.py:271
  30.5 5.0 %gather_fusion = f32[1024,10]{1,0:T(8,128)S(1)} fusion(f32[10,8192]{0,1:T(8,128)} %copy.23, s32[1024]{0:T(1024)S(1)} %broadcast_clamp_fusion), kind=kCustom, calls=%fused_computation | custom fusion | bytes 86016 | tf_op jit(solution)/shard_map/jit(_take)/gather | solution.py:274
  35.5 0.2 copy.24
  35.7 0.0 copy-done.1
  35.7 0.0 copy-done
  35.7 25.8 %leaf.1 = (f32[768,768]{1,0:T(8,128)S(1)}, f32[408,1024]{1,0:T(8,128)S(1)}, f32[840,128]{1,0:T(8,128)S(1)}) custom-call(s32[2]{0:T(128)S(1)} %pad_add_fusion.place_ref.refs_7_, f32[10,1024]{1,0:T(8,128)S(1)} %select_bitcast_fusion.data_ref, f32[8,1]{1,0:T(8,128)S(1)} %copy.25.length_ref, f32[7,8,128]{2,1,0:T(8,128)S(1)} %copy-done, f32[7,128]{1,0:T(8,128)S(1)} %copy-done.1, ...), custom_call_target="tpu_custom_call" | custom-call | tf_op jit(solution)/shard_map/leaf/pallas_call | solution.py:279
  61.5 0.3 collective-permute-start.7
  61.9 7.9 %collective-permute-done.7.other_ref = f32[840,128]{1,0:T(8,128)S(1)} collective-permute-done((f32[840,128]{1,0:T(8,128)S(1)}, f32[840,128]{1,0:T(8,128)S(1)}, u32[]{:S(2)}, u32[]{:S(2)}) %collective-permute-start.7) | collective-permute-done | bytes 430112 | tf_op jit(solution)/shard_map/ppermute | solution.py:26
  69.8 2.6 %height_1.1 = (f32[280,128]{1,0:T(8,128)S(1)}, f32[432,128]{1,0:T(8,128)S(1)}) custom-call(f32[840,128]{1,0:T(8,128)S(1)} %get-tuple-element.13.own_ref, f32[840,128]{1,0:T(8,128)S(1)} %collective-permute-done.7.other_ref), custom_call_target="tpu_custom_call" | custom-call | tf_op jit(solution)/shard_map/height_1/pallas_call | solution.py:301
  72.4 1.8 %collective-permute-start.8 = (f32[432,128]{1,0:T(8,128)S(1)}, f32[432,128]{1,0:T(8,128)S(1)}, u32[]{:S(2)}, u32[]{:S(2)}) collective-permute-start(f32[432,128]{1,0:T(8,128)S(1)} %get-tuple-element.14.own_ref), channel_id=1, source_target_pairs={{0,8},{4,12},{8,0},{12,4},{16,24},{20,28},{24,16},{28,20},{1,9},{5... | collective-permute-start | bytes 663560 | tf_op jit(solution)/shard_map/ppermute | solution.py:26
  74.2 4.2 %collective-permute-done.8.other_ref = f32[432,128]{1,0:T(8,128)S(1)} collective-permute-done((f32[432,128]{1,0:T(8,128)S(1)}, f32[432,128]{1,0:T(8,128)S(1)}, u32[]{:S(2)}, u32[]{:S(2)}) %collective-permute-start.8) | collective-permute-done | bytes 221216 | tf_op jit(solution)/shard_map/ppermute | solution.py:26
  78.4 2.6 %height_2.1 = (f32[152,128]{1,0:T(8,128)S(1)}, f32[152,128]{1,0:T(8,128)S(1)}) custom-call(f32[432,128]{1,0:T(8,128)S(1)} %get-tuple-element.14.own_ref, f32[432,128]{1,0:T(8,128)S(1)} %collective-permute-done.8.other_ref), custom_call_target="tpu_custom_call" | custom-call | tf_op jit(solution)/shard_map/height_2/pallas_call | solution.py:301
  81.0 2.8 %collective-permute-start.9 = (f32[152,128]{1,0:T(8,128)S(1)}, f32[152,128]{1,0:T(8,128)S(1)}, u32[]{:S(2)}, u32[]{:S(2)}) collective-permute-start(f32[152,128]{1,0:T(8,128)S(1)} %get-tuple-element.15.refs_0_), channel_id=1, source_target_pairs={{0,16},{4,20},{8,24},{12,28},{16,0},{20,4},{24,8},{28,12},{1,17},{... | collective-permute-start | bytes 233480 | tf_op jit(solution)/shard_map/ppermute | solution.py:26
  83.8 2.6 %collective-permute-done.9.refs_1_ = f32[152,128]{1,0:T(8,128)S(1)} collective-permute-done((f32[152,128]{1,0:T(8,128)S(1)}, f32[152,128]{1,0:T(8,128)S(1)}, u32[]{:S(2)}, u32[]{:S(2)}) %collective-permute-start.9) | collective-permute-done | bytes 77856 | tf_op jit(solution)/shard_map/ppermute | solution.py:26
  86.4 5.6 %final.1 = (f32[1,1024]{1,0:T(1,128)}, f32[16,1024]{1,0:T(8,128)}, f32[1,1024]{1,0:T(1,128)S(1)}) custom-call(f32[152,128]{1,0:T(8,128)S(1)} %get-tuple-element.15.refs_0_, f32[152,128]{1,0:T(8,128)S(1)} %collective-permute-done.9.refs_1_, f32[280,128]{1,0:T(8,128)S(1)} %get-tuple-element.16.refs_2_, f32[152,128]{1,0:T(8,128)S(1)} %get-tuple-element.17.refs_3_, ...), custom_call_target="tpu_custom_call" | custom-call | tf_op jit(solution)/shard_map/final/pallas_call | solution.py:315
  92.0 0.0 collective-permute-start.10
  92.0 1.2 %collective-permute-done.10 = f32[1,1024]{1,0:T(1,128)S(1)} collective-permute-done((f32[1,1024]{1,0:T(1,128)S(1)}, f32[1,1024]{1,0:T(1,128)S(1)}, u32[]{:S(2)}, u32[]{:S(2)}) %collective-permute-start.10) | collective-permute-done | bytes 4128 | tf_op jit(solution)/shard_map/ppermute | solution.py:26
  93.1 1.5 %collective-permute-start.11 = (f32[1,1024]{1,0:T(1,128)S(1)}, f32[1,1024]{1,0:T(1,128)S(1)}, u32[]{:S(2)}, u32[]{:S(2)}) collective-permute-start(f32[1,1024]{1,0:T(1,128)S(1)} %add.20), channel_id=1, source_target_pairs={{0,2},{1,3},{2,0},{3,1},{4,6},{5,7},{6,4},{7,5},{8,10},{9,11},{10,... | collective-permute-start | bytes 12296 | tf_op jit(solution)/shard_map/ppermute | solution.py:26
  94.7 2.1 %collective-permute-done.11 = f32[1,1024]{1,0:T(1,128)S(1)} collective-permute-done((f32[1,1024]{1,0:T(1,128)S(1)}, f32[1,1024]{1,0:T(1,128)S(1)}, u32[]{:S(2)}, u32[]{:S(2)}) %collective-permute-start.11) | collective-permute-done | bytes 4128 | tf_op jit(solution)/shard_map/ppermute | solution.py:26
  96.7 1.3 %fusion = f32[1024]{0:T(1024)} fusion(f32[1024]{0:T(1024)S(1)} %bitcast.10, f32[1024]{0:T(1024)} %bitcast.13), kind=kLoop, calls=%fused_computation.13 | loop fusion | flops 3072 | bytes 12288 | tf_op jit(solution)/shard_map/sub | solution.py:331
  (10 shorter events, 0.1 us)
Async XLA Ops:
  0.6 35.1 %copy-start.1 = (f32[7,128]{1,0:T(8,128)S(1)}, f32[7,128]{1,0:T(8,128)}, u32[]{:S(2)}) copy-start(f32[7,128]{1,0:T(8,128)} %phase_ref.1) | copy-start | bytes 10756
  0.6 35.1 %copy-start = (f32[7,8,128]{2,1,0:T(8,128)S(1)}, f32[7,8,128]{2,1,0:T(8,128)}, u32[]{:S(2)}) copy-start(f32[7,8,128]{2,1,0:T(8,128)} %frequency_ref.1) | copy-start | bytes 86020
  1.5 22.2 %collective-permute-start.5 = (f32[10,1024]{1,0:T(8,128)S(1)}, f32[10,1024]{1,0:T(8,128)S(1)}, u32[]{:S(2)}, u32[]{:S(2)}) collective-permute-start(f32[10,1024]{1,0:T(8,128)S(1)} %get-tuple-element.23), channel_id=1, source_target_pairs={{0,24},{4,28},{8,0},{12,4},{16,8},{20,12},{24,16},{28,20},{1,25},{... | collective-permute-start | bytes 122888 | tf_op jit(solution)/shard_map/ppermute | solution.py:270
  6.6 17.1 %collective-permute-start.4 = (f32[10,1024]{1,0:T(8,128)S(1)}, f32[10,1024]{1,0:T(8,128)S(1)}, u32[]{:S(2)}, u32[]{:S(2)}) collective-permute-start(f32[10,1024]{1,0:T(8,128)S(1)} %get-tuple-element.23), channel_id=1, source_target_pairs={{0,20},{4,24},{8,28},{12,0},{16,4},{20,8},{24,12},{28,16},{1,21},{... | collective-permute-start | bytes 122888 | tf_op jit(solution)/shard_map/ppermute | solution.py:270
  6.9 16.7 %collective-permute-start.3 = (f32[10,1024]{1,0:T(8,128)S(1)}, f32[10,1024]{1,0:T(8,128)S(1)}, u32[]{:S(2)}, u32[]{:S(2)}) collective-permute-start(f32[10,1024]{1,0:T(8,128)S(1)} %get-tuple-element.23), channel_id=1, source_target_pairs={{0,16},{4,20},{8,24},{12,28},{16,0},{20,4},{24,8},{28,12},{1,17},{... | collective-permute-start | bytes 122888 | tf_op jit(solution)/shard_map/ppermute | solution.py:270
  10.4 13.2 %collective-permute-start.2 = (f32[10,1024]{1,0:T(8,128)S(1)}, f32[10,1024]{1,0:T(8,128)S(1)}, u32[]{:S(2)}, u32[]{:S(2)}) collective-permute-start(f32[10,1024]{1,0:T(8,128)S(1)} %get-tuple-element.23), channel_id=1, source_target_pairs={{0,12},{4,16},{8,20},{12,24},{16,28},{20,0},{24,4},{28,8},{1,13},{... | collective-permute-start | bytes 122888 | tf_op jit(solution)/shard_map/ppermute | solution.py:270
  10.4 7.1 %collective-permute-start = (f32[10,1024]{1,0:T(8,128)S(1)}, f32[10,1024]{1,0:T(8,128)S(1)}, u32[]{:S(2)}, u32[]{:S(2)}) collective-permute-start(f32[10,1024]{1,0:T(8,128)S(1)} %get-tuple-element.23), channel_id=1, source_target_pairs={{0,4},{4,8},{8,12},{12,16},{16,20},{20,24},{24,28},{28,0},{1,5},{5... | collective-permute-start | bytes 122888 | tf_op jit(solution)/shard_map/ppermute | solution.py:270
  17.5 6.1 %collective-permute-start.1 = (f32[10,1024]{1,0:T(8,128)S(1)}, f32[10,1024]{1,0:T(8,128)S(1)}, u32[]{:S(2)}, u32[]{:S(2)}) collective-permute-start(f32[10,1024]{1,0:T(8,128)S(1)} %get-tuple-element.23), channel_id=1, source_target_pairs={{0,8},{4,12},{8,16},{12,20},{16,24},{20,28},{24,0},{28,4},{1,9},{5... | collective-permute-start | bytes 122888 | tf_op jit(solution)/shard_map/ppermute | solution.py:270
  23.6 4.3 %collective-permute-start.6 = (f32[10,1024]{1,0:T(8,128)S(1)}, f32[10,1024]{1,0:T(8,128)S(1)}, u32[]{:S(2)}, u32[]{:S(2)}) collective-permute-start(f32[10,1024]{1,0:T(8,128)S(1)} %get-tuple-element.23), channel_id=1, source_target_pairs={{0,28},{4,0},{8,4},{12,8},{16,12},{20,16},{24,20},{28,24},{1,29},{... | collective-permute-start | bytes 122888 | tf_op jit(solution)/shard_map/ppermute | solution.py:270
  61.5 8.2 %collective-permute-start.7 = (f32[840,128]{1,0:T(8,128)S(1)}, f32[840,128]{1,0:T(8,128)S(1)}, u32[]{:S(2)}, u32[]{:S(2)}) collective-permute-start(f32[840,128]{1,0:T(8,128)S(1)} %get-tuple-element.13.own_ref), channel_id=1, source_target_pairs={{0,4},{4,0},{8,12},{12,8},{16,20},{20,16},{24,28},{28,24},{1,5},{5... | collective-permute-start | bytes 1290248 | tf_op jit(solution)/shard_map/ppermute | solution.py:26
  72.4 6.0 %collective-permute-start.8 = (f32[432,128]{1,0:T(8,128)S(1)}, f32[432,128]{1,0:T(8,128)S(1)}, u32[]{:S(2)}, u32[]{:S(2)}) collective-permute-start(f32[432,128]{1,0:T(8,128)S(1)} %get-tuple-element.14.own_ref), channel_id=1, source_target_pairs={{0,8},{4,12},{8,0},{12,4},{16,24},{20,28},{24,16},{28,20},{1,9},{5... | collective-permute-start | bytes 663560 | tf_op jit(solution)/shard_map/ppermute | solution.py:26
  81.0 5.4 %collective-permute-start.9 = (f32[152,128]{1,0:T(8,128)S(1)}, f32[152,128]{1,0:T(8,128)S(1)}, u32[]{:S(2)}, u32[]{:S(2)}) collective-permute-start(f32[152,128]{1,0:T(8,128)S(1)} %get-tuple-element.15.refs_0_), channel_id=1, source_target_pairs={{0,16},{4,20},{8,24},{12,28},{16,0},{20,4},{24,8},{28,12},{1,17},{... | collective-permute-start | bytes 233480 | tf_op jit(solution)/shard_map/ppermute | solution.py:26
  92.0 1.2 %collective-permute-start.10 = (f32[1,1024]{1,0:T(1,128)S(1)}, f32[1,1024]{1,0:T(1,128)S(1)}, u32[]{:S(2)}, u32[]{:S(2)}) collective-permute-start(f32[1,1024]{1,0:T(1,128)S(1)} %get-tuple-element.22), channel_id=1, source_target_pairs={{0,1},{1,0},{2,3},{3,2},{4,5},{5,4},{6,7},{7,6},{8,9},{9,8},{10,11... | collective-permute-start | bytes 12296 | tf_op jit(solution)/shard_map/ppermute | solution.py:26
  93.1 3.6 %collective-permute-start.11 = (f32[1,1024]{1,0:T(1,128)S(1)}, f32[1,1024]{1,0:T(1,128)S(1)}, u32[]{:S(2)}, u32[]{:S(2)}) collective-permute-start(f32[1,1024]{1,0:T(1,128)S(1)} %add.20), channel_id=1, source_target_pairs={{0,2},{1,3},{2,0},{3,1},{4,6},{5,7},{6,4},{7,5},{8,10},{9,11},{10,... | collective-permute-start | bytes 12296 | tf_op jit(solution)/shard_map/ppermute | solution.py:26

commit v2 on v1

v2 whole, which is shorter than its diff:
```python
import functools
import math

import jax
import jax.numpy as jnp
from jax import lax
from jax.experimental import pallas as pl
from jax.experimental.pallas import tpu as pltpu
from jax.sharding import PartitionSpec as P

PROBES = 64
BLOCK = 256
SETTLED = 1.001
SHARES = ((3, 3, 3, 3, 3), (2, 2, 2, 2, 2))

f32 = jnp.float32
bf16 = jnp.bfloat16
highest = lax.Precision.HIGHEST
hash_first = 747796405
hash_second = -1403630843
hash_third = -2073254261
VMEM_BYTES = 40 * 1024 * 1024


def partner_of(block, axis, apart):
    count = lax.axis_size(axis)
    return lax.ppermute(block, axis, [(i, i ^ (1 << apart)) for i in range(count)])


def halves(x):
    high = x.astype(bf16)
    return high, (x - high.astype(f32)).astype(bf16)


def thirds(x):
    high = x.astype(bf16)
    rest = x - high.astype(f32)
    middle = rest.astype(bf16)
    return high, middle, (rest - middle.astype(f32)).astype(bf16)


NN = (((1,), (0,)), ((), ()))
NT = (((1,), (1,)), ((), ()))
TN = (((0,), (0,)), ((), ()))


def dot_one(a, b, dims=NN):
    return lax.dot_general(a, b, dims, preferred_element_type=f32)


def dot_three(a, b, dims=NN):
    a_high, a_low = halves(a)
    b_high, b_low = halves(b)
    return dot_one(a_high, b_high, dims) + (dot_one(a_high, b_low, dims) + dot_one(a_low, b_high, dims))


def dot_full(a, b, dims=NN):
    return lax.dot_general(a, b, dims, precision=highest, preferred_element_type=f32)


def unit(size):
    rows = lax.broadcasted_iota(jnp.int32, (size, size), 0)
    columns = lax.broadcasted_iota(jnp.int32, (size, size), 1)
    return rows == columns


def gain(ratio):
    reach = (ratio - 1.0) / (ratio + 1.0)
    return 2.0 / (2.0 - reach * reach)


def tighter(ratio):
    return (ratio + 1.0) * (ratio + 1.0) / (4.0 * ratio)


def no_work(count):
    pass


def inverse(matrix, low, residual, approx, other_work=no_work, share=(0, 0, 0, 0, 0)):
    size = matrix.shape[0]
    same = unit(size)
    high = jnp.max(jnp.sum(jnp.abs(matrix), axis=0, keepdims=True)) * 1.0001
    low = jnp.minimum(low, high) * 0.9999
    scale = 2.0 / (low + high)
    ratio = high / low
    c = gain(ratio)
    first = jnp.where(same, 1.0, 0.0) - scale * matrix
    residual[...] = c * dot_three(first, first) - jnp.where(same, c - 1.0, 0.0)
    approx[...] = (c * scale) * (first + jnp.where(same, 1.0, 0.0))
    ratio = tighter(ratio)
    other_work(share[0])

    def more(ratio):
        return tighter(ratio) > SETTLED

    def double(ratio):
        c = gain(ratio)
        e = residual[...]
        x = approx[...]
        squared = dot_three(e, e)
        moved = dot_three(x, e)
        residual[...] = c * squared - jnp.where(same, c - 1.0, 0.0)
        approx[...] = c * (x + moved)
        return tighter(ratio)

    for step in (1, 2):
        ratio = double(ratio)
        other_work(share[step])
    ratio = lax.while_loop(more, double, ratio)
    x = approx[...]
    x = gain(ratio) * (x + dot_three(x, residual[...]))
    other_work(share[3])
    left = jnp.where(same, 1.0, 0.0) - dot_full(x, matrix)
    other_work(share[4])
    return x + dot_three(left, x)


def cosine(x):
    turns = jnp.floor(x * (1.0 / math.pi) + 0.5)
    r = x - turns * 3.140625
    r = r - turns * 9.67502593994140625e-4
    r = r - turns * 1.509957990978376e-7
    odd = jnp.bitwise_and(turns.astype(jnp.int32), 1)
    s = r * r
    value = 1.0 / 479001600.0
    for term in (-1.0 / 3628800.0, 1.0 / 40320.0, -1.0 / 720.0, 1.0 / 24.0, -0.5, 1.0):
        value = value * s + term
    return jnp.where(odd == 1, -value, value)


def logical_right(x, by):
    return lax.shift_right_logical(x, jnp.full_like(x, by))


def signs_of(seeds, positions):
    mixed = seeds * jnp.int32(hash_first) + positions * jnp.int32(hash_second)
    mixed = jnp.bitwise_xor(mixed, logical_right(mixed, 15))
    mixed = mixed * jnp.int32(hash_third)
    mixed = jnp.bitwise_xor(mixed, logical_right(mixed, 13))
    parity = jnp.bitwise_and(logical_right(mixed, 11), jnp.full_like(mixed, 1))
    return (2 * parity - 1).astype(f32)


def fetch(half_and_covs, code, lane, near_ref, far_ref):
    chunks, lanes = code.shape
    half, covs = half_and_covs
    shape = (covs, lanes)
    codes = [jnp.broadcast_to(code[k:k + 1], shape) for k in range(chunks)]
    places = [jnp.broadcast_to(lane[k:k + 1], shape) for k in range(chunks)]
    down = lax.broadcasted_iota(jnp.int32, (chunks, lanes), 0)
    zero = jnp.zeros(shape, f32)

    def from_side(ref, side, totals):
        def from_piece(piece, totals):
            coords, targets, noise = [list(t) for t in totals]
            number = (side * half + piece) * chunks
            start = pl.multiple_of(piece * (chunks * (covs + 2)), 8)
            for c in range(chunks):
                source = ref[pl.ds(start + c * covs, covs), :]
                for k in range(chunks):
                    coords[k] = jnp.where(codes[k] == number + c, jnp.take_along_axis(source, places[k], axis=1), coords[k])
            for at, found in ((chunks * covs, targets), (chunks * (covs + 1), noise)):
                source = ref[pl.ds(start + at, chunks), :]
                for k in range(chunks):
                    found[k] = jnp.where(codes[k] == number + down, jnp.take_along_axis(source, places[k], axis=1), found[k])
            return tuple(coords), tuple(targets), tuple(noise)

        return lax.fori_loop(0, half, from_piece, totals)

    totals = ((zero,) * chunks,) * 3
    totals = from_side(far_ref, 1, from_side(near_ref, 0, totals))
    coords, targets, noise = totals
    return (
        jnp.concatenate(coords, axis=1),
        jnp.concatenate([jnp.sum(t, axis=0, keepdims=True) for t in targets], axis=1),
        jnp.concatenate([jnp.sum(t, axis=0, keepdims=True) for t in noise], axis=1),
    )


def down(row, count):
    shape = (count, row.shape[1])
    same = lax.broadcasted_iota(jnp.int32, shape, 0) == lax.broadcasted_iota(jnp.int32, shape, 1)
    return jnp.sum(jnp.where(same, jnp.broadcast_to(row, shape), jnp.zeros(shape, row.dtype)), axis=1, keepdims=True)


def early_kernel(levels, nodes, place_ref, whole_ref, real_ref, code_ref, lane_ref, scale_ref, wave_ref, sign_ref):
    chunks, lanes = code_ref.shape
    covs = scale_ref.shape[0]
    leaf = place_ref[0]
    half = 1 << (levels - 1)
    order = whole_ref[:chunks, :]
    owner = jnp.right_shift(order, (chunks * lanes).bit_length() - 1)
    chunk = jnp.bitwise_and(jnp.right_shift(order, lanes.bit_length() - 1), chunks - 1)
    across = jnp.bitwise_and(jnp.bitwise_xor(owner, leaf), 1)
    turn = jnp.bitwise_and(jnp.right_shift(jnp.bitwise_xor(leaf, across) - owner, 1), half - 1)
    code_ref[...] = (across * half + turn) * chunks + chunk
    lane_ref[...] = jnp.bitwise_and(order, lanes - 1)
    scale_ref[...] = jnp.broadcast_to(down(real_ref[nodes * (covs + 1):nodes * (covs + 1) + 1, :], covs), scale_ref.shape)
    rank = wave_ref.shape[2]
    at_row = lax.broadcasted_iota(jnp.int32, (8, rank), 0)
    for level in range(levels):
        node = jnp.right_shift((1 << levels) + leaf, level + 1) - 1
        fh, fm, fl = [p.astype(f32) for p in thirds(real_ref[pl.ds(pl.multiple_of(node * covs, covs), covs), :])]
        ph, pm, p_low = [p.astype(f32) for p in thirds(real_ref[pl.ds(nodes * covs + node, 1), :])]
        phases = jnp.where(at_row == 0, ph, jnp.where(at_row == 1, pm, jnp.where(at_row == 2, p_low, 0.0)))
        wave_ref[level] = jnp.concatenate([fh, fh, fm, fm, fh, fl, phases, jnp.zeros_like(phases)], axis=0)
    probes, width = sign_ref.shape
    positions = leaf * width + lax.broadcasted_iota(jnp.int32, (probes, width), 1)
    sign_ref[...] = signs_of(down(whole_ref[chunks:chunks + 1, :], probes), positions)


def leaf_kernel(levels, code_ref, lane_ref, scale_ref, wave_ref, sign_ref, near_ref, far_ref,
                lower_ref, aug_ref, first_ref, rest_ref, matrix, inverses, residual, approx):
    probes, width = sign_ref.shape
    rank = wave_ref.shape[2]
    covs = scale_ref.shape[0]
    blocks = width // BLOCK
    top = width + levels * rank
    coords, targets, noise = fetch((1 << (levels - 1), covs), code_ref[...], lane_ref[...], near_ref, far_ref)
    u = coords / scale_ref[:, :1]
    s = -0.5 * jnp.sum(u * u, axis=0, keepdims=True)
    rows = matrix.shape[0]
    h, m, l = [p.astype(f32) for p in thirds(u)]
    row = lax.broadcasted_iota(jnp.int32, (8, width), 0)
    ones = jnp.where(row < 3, 1.0, 0.0)
    same = unit(BLOCK)
    spans = [slice(k * BLOCK, (k + 1) * BLOCK) for k in range(blocks)]
    side_ranges = [(start, min(start + BLOCK, rows)) for start in range(width, rows, BLOCK)]
    leaf_ranges = [(k * BLOCK, (k + 1) * BLOCK) for k in range(blocks)]
    s_parts = [p.astype(f32) for p in thirds(s)]
    s_rows = jnp.where(row == 0, s_parts[0], jnp.where(row == 1, s_parts[1], jnp.where(row == 2, s_parts[2], 0.0)))
    left_points = jnp.concatenate([h, h, m, m, h, l, s_rows, ones], axis=0).astype(bf16)
    right_points = jnp.concatenate([h, m, h, m, l, h, ones, s_rows], axis=0).astype(bf16)
    basis_points = jnp.concatenate([h, m, h, m, l, h, ones, ones], axis=0).astype(bf16)

    def build(i, j):
        part = jnp.exp(dot_one(left_points[:, spans[i]], right_points[:, spans[j]], TN))
        if i == j:
            part = part + jnp.where(same, noise[:, spans[i]], 0.0)
        matrix[spans[i], spans[j]] = part

    def basis(level):
        angle = dot_one(wave_ref[level].astype(bf16), basis_points, TN)
        matrix[width + level * rank:width + (level + 1) * rank, :] = math.sqrt(2.0 / rank) * cosine(angle)

    def right_sides():
        matrix[top:top + probes, :] = sign_ref[...]
        matrix[top + probes:, :] = jnp.concatenate([targets, jnp.zeros((rows - top - probes - 1, width), f32)], axis=0)

    def weights_at(rows_of, k):
        start, end = rows_of
        if start < width:
            return lower_ref.at[start - BLOCK:end - BLOCK, spans[k]]
        return aug_ref.at[start - width:end - width, spans[k]]

    def weigh(rows_of, k):
        weights_at(rows_of, k)[...] = dot_full(matrix[rows_of[0]:rows_of[1], spans[k]], inverses[k % 2])

    def update(rows_of, j, k):
        here = slice(*rows_of)
        matrix[here, spans[j]] = matrix[here, spans[j]] - dot_full(weights_at(rows_of, k)[...], matrix[spans[j], spans[k]], NT)

    def add_up(level, k):
        many = min(2, levels - level)
        start = level * rank
        columns = matrix[width + start:width + start + many * rank, spans[k]]
        part = dot_full(aug_ref[start:, spans[k]], columns, NT)
        for next_to in range(many):
            column = level + next_to
            at = sum(rows - width - before * rank for before in range(1, column))
            count = rows - width - column * rank
            piece = part[next_to * rank:, next_to * rank:(next_to + 1) * rank]
            kept = (rest_ref if column else first_ref).at[at:at + count, :]
            kept[...] = piece if k == 0 else kept[...] + piece

    tasks, done, queue = {}, set(), []

    def add(key, call, after=()):
        tasks[key] = (call, after)
        queue.append(key)

    def run(key):
        if key not in done:
            done.add(key)
            call, after = tasks[key]
            for other in after:
                run(other)
            call()

    def other_work(count):
        while count and queue:
            key = queue.pop(0)
            if key not in done:
                run(key)
                count -= 1

    def ready(rows_of, j, k):
        if rows_of[0] < width:
            first = [("build", rows_of[0] // BLOCK, j)]
        else:
            first = [("basis", level) for level in range(levels)] + [("right",)]
        return first + [("update", rows_of, j, before) for before in range(k)]

    for j in range(blocks):
        for i in range(j, blocks):
            add(("build", i, j), functools.partial(build, i, j))
        if j == 0:
            for level in range(levels):
                add(("basis", level), functools.partial(basis, level))
            add(("right",), right_sides)
    for k in range(blocks):
        for key in ready(leaf_ranges[k], k, k):
            run(key)
        found = inverse(matrix[spans[k], spans[k]], jnp.min(noise[:, spans[k]]), residual, approx, other_work, SHARES[min(k, 1)])
        if k > 1:
            for key in tasks:
                if key[0] == "weigh" and key[2] == k - 2:
                    run(key)
        inverses[k % 2] = found
        ranges = leaf_ranges[k + 1:] + side_ranges
        for rows_of in ranges:
            add(("weigh", rows_of, k), functools.partial(weigh, rows_of, k), ready(rows_of, k, k))
        for j in range(k + 1, blocks):
            for rows_of in leaf_ranges[j:] + side_ranges:
                add(("update", rows_of, j, k), functools.partial(update, rows_of, j, k),
                    ready(rows_of, j, 0) + ready(leaf_ranges[j], k, k) + [("weigh", rows_of, k)])
        for level in range(0, levels, 2):
            add(("sum", level, k), functools.partial(add_up, level, k),
                [("weigh", rows_of, k) for rows_of in side_ranges]
                + [key for rows_of in side_ranges for key in ready(rows_of, k, k)])
    other_work(len(queue))


def eliminate(own, other, rank, residual, approx):
    total = own + other
    capacitance = total[:rank] + jnp.where(unit(rank), 1.0, 0.0)
    return total, dot_full(total[rank:], inverse(capacitance, jnp.float32(1.0), residual, approx))


def height_kernel(own_ref, other_ref, coefficient_ref, total_ref, residual, approx):
    total, coefficients = eliminate(own_ref[...], other_ref[...], own_ref.shape[1], residual, approx)
    coefficient_ref[...] = coefficients
    total_ref[...] = total[own_ref.shape[1]:]


def reduce_kernel(left, coefficient_ref, total_ref, own_ref, other_ref, *out_refs):
    rank = own_ref.shape[1]
    at = to = 0
    for level in range(1, left):
        start = (level - 1) * rank
        size = coefficient_ref.shape[0] - start
        value = own_ref[at:at + size, :] + other_ref[at:at + size, :] - dot_full(
            coefficient_ref[start:, :], total_ref[start:start + rank, :], NT)
        if level == 1:
            out_refs[0][...] = value
        else:
            out_refs[1][to:to + size, :] = value
            to += size
        at += size


def back_kernel(lower_ref, aug_ref, solved_ref):
    width = aug_ref.shape[1]
    spans = [slice(k * BLOCK, (k + 1) * BLOCK) for k in range(width // BLOCK)]
    for k in range(len(spans) - 1, -1, -1):
        value = aug_ref[:, spans[k]]
        for j in range(k + 1, len(spans)):
            value = value - dot_full(solved_ref[:, spans[j]], lower_ref[(j - 1) * BLOCK:j * BLOCK, spans[k]])
        solved_ref[:, spans[k]] = value


def apply_kernel(coefficient_ref, solved_ref, rest_ref):
    rank = coefficient_ref.shape[1]
    rest_ref[...] = solved_ref[rank:, :] - dot_full(coefficient_ref[...], solved_ref[:rank, :])


def final_kernel(own_ref, other_ref, solved_ref, sign_ref, target_ref, solve_ref, terms_ref, residual, approx):
    rank = own_ref.shape[1]
    probes = sign_ref.shape[0]
    _, last = eliminate(own_ref[...], other_ref[...], rank, residual, approx)
    solved = solved_ref[rank:, :] - dot_full(last, solved_ref[:rank, :])
    solve_ref[...] = solved[:probes]
    target_ref[...] = solved[probes:probes + 1]
    terms_ref[...] = jnp.sum(sign_ref[...] * solved[:probes], axis=0, keepdims=True)


def whole(count=1):
    return [pl.BlockSpec(memory_space=pltpu.VMEM)] * count


def scalars():
    return pl.BlockSpec(memory_space=pltpu.SMEM)


def shards(covariates, targets, noise_var, lengths, frequencies, phases, tree_order, probe_seeds):
    leaf_count = lax.axis_size("leaf")
    leaf_index = lax.axis_index("leaf")
    width = tree_order.shape[0]
    rank = phases.shape[1]
    probes = probe_seeds.shape[0]
    levels = leaf_count.bit_length() - 1
    tail = -(-(probes + 1) // 8) * 8
    lanes = 128
    chunks = width // lanes
    covs = covariates.shape[0]
    piece = jnp.concatenate(
        [
            covariates.reshape(covs, chunks, lanes).transpose(1, 0, 2).reshape(chunks * covs, lanes),
            targets.reshape(chunks, lanes),
            noise_var.reshape(chunks, lanes),
        ],
        axis=0,
    )
    piece = lax.optimization_barrier(piece)
    pieces = [piece]
    for k in range(2, leaf_count, 2):
        pieces.append(lax.ppermute(piece, "leaf", [(i, (i + k) % leaf_count) for i in range(leaf_count)]))
    near = jnp.concatenate(pieces, axis=0)
    place = leaf_index[None].astype(jnp.int32)
    sizes = [(levels - level) * rank + tail for level in range(levels)]
    params = pltpu.CompilerParams(vmem_limit_bytes=VMEM_BYTES)
    nodes = phases.shape[0]
    integers = jnp.concatenate([tree_order.reshape(chunks, lanes), jnp.pad(probe_seeds, (0, lanes - probes))[None]], axis=0)
    reals = jnp.concatenate([frequencies.reshape(nodes * covs, rank), phases, jnp.pad(lengths, (0, rank - covs))[None]], axis=0)
    code, lane, scale, waves, signs = pl.pallas_call(
        functools.partial(early_kernel, levels, nodes),
        out_shape=(
            jax.ShapeDtypeStruct((chunks, lanes), jnp.int32),
            jax.ShapeDtypeStruct((chunks, lanes), jnp.int32),
            jax.ShapeDtypeStruct((covs, lanes), f32),
            jax.ShapeDtypeStruct((levels, 8 * covs, rank), f32),
            jax.ShapeDtypeStruct((probes, width), f32),
        ),
        in_specs=[scalars()] + whole(2),
        out_specs=tuple(whole(5)),
        compiler_params=params,
        name="early",
    )(place, integers, reals)
    near, code, lane, scale, waves, signs = lax.optimization_barrier((near, code, lane, scale, waves, signs))
    far = partner_of(near, "leaf", 0)
    side = levels * rank + tail
    lower, aug, first, later = pl.pallas_call(
        functools.partial(leaf_kernel, levels),
        out_shape=(
            jax.ShapeDtypeStruct((width - BLOCK, width - BLOCK), f32),
            jax.ShapeDtypeStruct((side, width), f32),
            jax.ShapeDtypeStruct((sizes[0], rank), f32),
            jax.ShapeDtypeStruct((sum(sizes[1:]), rank), f32),
        ),
        in_specs=whole(7),
        out_specs=tuple(whole(4)),
        scratch_shapes=[
            pltpu.VMEM((width + side, width), f32),
            pltpu.VMEM((2, BLOCK, BLOCK), f32),
            pltpu.VMEM((BLOCK, BLOCK), f32),
            pltpu.VMEM((BLOCK, BLOCK), f32),
        ],
        compiler_params=params,
        name="leaf",
    )(code, lane, scale, waves, signs, near, far)
    small = [pltpu.VMEM((rank, rank), f32), pltpu.VMEM((rank, rank), f32)]
    solved = pl.pallas_call(
        back_kernel,
        out_shape=jax.ShapeDtypeStruct((side, width), f32),
        in_specs=whole(2),
        out_specs=whole()[0],
        compiler_params=params,
        cost_estimate=pl.CostEstimate(flops=12 * side * width * width // 2, bytes_accessed=0, transcendentals=0),
        name="back",
    )(lower, aug)
    for height in range(1, levels):
        left = levels - height + 1
        other_first = partner_of(first, "leaf", height - 1)
        other_later = partner_of(later, "leaf", height - 1)
        other_first, solved = lax.optimization_barrier((other_first, solved))
        rest = side - height * rank
        coefficient, total = pl.pallas_call(
            height_kernel,
            out_shape=(jax.ShapeDtypeStruct((rest, rank), f32), jax.ShapeDtypeStruct((rest, rank), f32)),
            in_specs=whole(2),
            out_specs=tuple(whole(2)),
            scratch_shapes=small,
            compiler_params=params,
            name=f"height_{height}",
        )(first, other_first)
        outs = [jax.ShapeDtypeStruct((sizes[height], rank), f32)]
        if left > 2:
            outs.append(jax.ShapeDtypeStruct((sum(sizes[height + 1:]), rank), f32))
        found = pl.pallas_call(
            functools.partial(reduce_kernel, left),
            out_shape=tuple(outs),
            in_specs=whole(4),
            out_specs=tuple(whole(len(outs))),
            compiler_params=params,
            name=f"reduce_{height}",
        )(coefficient, total, later, other_later)
        first, later = found[0], found[-1]
        solved = pl.pallas_call(
            apply_kernel,
            out_shape=jax.ShapeDtypeStruct((rest, width), f32),
            in_specs=whole(2),
            out_specs=whole()[0],
            compiler_params=params,
            cost_estimate=pl.CostEstimate(flops=12 * rest * rank * width, bytes_accessed=0, transcendentals=0),
            name=f"apply_{height}",
        )(coefficient, solved)
    other = partner_of(first, "leaf", levels - 1)
    target_solve, probe_solves, terms = pl.pallas_call(
        final_kernel,
        out_shape=(
            jax.ShapeDtypeStruct((1, width), f32),
            jax.ShapeDtypeStruct((probes, width), f32),
            jax.ShapeDtypeStruct((1, width), f32),
        ),
        in_specs=whole(4),
        out_specs=tuple(whole(3)),
        scratch_shapes=small,
        compiler_params=params,
        name="final",
    )(first, other, solved, signs)
    probe_count = lax.axis_size("probe")
    shared = [terms] + [
        lax.ppermute(terms, "probe", [(i, (i + k) % probe_count) for i in range(probe_count)]) for k in range(1, probe_count)
    ]
    target_solve = target_solve[0]
    estimate = functools.reduce(jnp.add, [t[0] for t in shared]) / PROBES
    noise_grad = 0.5 * target_solve * target_solve - 0.5 * estimate
    return (target_solve, probe_solves, noise_grad)


def solution(mesh):
    in_specs = (P(None, "leaf"), P("leaf"), P("leaf"), P(), P(), P(), P("leaf"), P("probe"))
    out_specs = (P("leaf"), P("probe", "leaf"), P("leaf"))
    return jax.shard_map(shards, mesh=mesh, in_specs=in_specs, out_specs=out_specs, check_vma=False)
```

time: 99 us -> 73.5 us (0.74)
  waiting for transfers between devices: 30.9 us -> 16.5 us
  local copies, waits for them, and re-layouts: 9.34 us -> 1.31 us
  starting transfers between devices: 16.8 us -> 15.2 us
    ppermute x7 -> x6, waiting for transfers between devices: 12.9 us -> 4.69 us  [the longest x3 2.8 us: shards(): lax.ppermute(terms, 'probe', [(i, (i + k) % probe_count) for i in range(p...]
    ppermute x5 -> x6, waiting for transfers between devices: 17.9 us -> 11.9 us  [partner_of(): lax.ppermute(block, axis, [(i, i ^ 1 << apart) for i in range(count)])]
    gather x2 -> x0, local copies, waits for them, and re-layouts: 5.18 us -> none  [shards(): data = jnp.take(gathered, place, axis=1)]
    concatenate x2 -> x0, local copies, waits for them, and re-layouts: 2.65 us -> none  [shards(): gathered = jnp.concatenate(pieces, axis=1)]
    ppermute x7 -> x6, starting transfers between devices: 10.4 us -> 7.8 us  [the longest x3 6.06 us: shards(): lax.ppermute(piece, 'leaf', [(i, (i + k) % leaf_count) for i in range(lea...]
    pallas_call x1, Pallas kernels: 25.8 us -> 23.4 us  [shards(): pl.pallas_call(functools.partial(leaf_kernel, levels), out_shape=(jax.Sha...]
    pallas_call x3 -> x9, Pallas kernels: 10.8 us -> 12.4 us  [the longest x2 3.86 us: shards(): pl.pallas_call(height_kernel, out_shape=(jax.ShapeDtypeStruct((rest, rank...]
    concatenate x1 -> x4, other arithmetic: 0.81 us -> 2.27 us  [the longest x1 0.8 us: shards(): jnp.concatenate([covariates.reshape(covs, chunks, lanes).transpose(1, 0,...]
  transfers between devices with their start and end apart: 12 -> 12, of which waited for: 8 -> 9; matrix products, arithmetic and copies ran while one was open for 3% -> 4% of each run, Pallas kernels for 0% -> 12%
where the time goes in v2:
time: 73.5 us; the launch traced here: 73.1 us
  Pallas kernels  35.8 us (49%)
  waiting for transfers between devices  16.5 us (22%)
  starting transfers between devices  15.2 us (21%)
  other arithmetic  3.57 us (5%)
  local copies, waits for them, and re-layouts  1.31 us (2%)
    pallas_call x1, Pallas kernels, shards(): pl.pallas_call(functools.partial(leaf_kernel, levels), out_shape=(jax.Sha...  23.4 us
    ppermute x6, waiting for transfers between devices, partner_of(): lax.ppermute(block, axis, [(i, i ^ 1 << apart) for i in range(count)])  11.9 us
    ppermute x6, starting transfers between devices, partner_of(): lax.ppermute(block, axis, [(i, i ^ 1 << apart) for i in range(count)])  7.38 us
    ppermute x3, starting transfers between devices, shards(): lax.ppermute(piece, 'leaf', [(i, (i + k) % leaf_count) for i in range(lea...  6.06 us
    pallas_call x2, Pallas kernels, shards(): pl.pallas_call(height_kernel, out_shape=(jax.ShapeDtypeStruct((rest, rank...  3.86 us
    pallas_call x1, Pallas kernels, shards(): pl.pallas_call(final_kernel, out_shape=(jax.ShapeDtypeStruct((1, width),...  3 us
    pallas_call x1, Pallas kernels, shards(): pl.pallas_call(back_kernel, out_shape=jax.ShapeDtypeStruct((side, width),...  2.92 us
    ppermute x3, waiting for transfers between devices, shards(): lax.ppermute(terms, 'probe', [(i, (i + k) % probe_count) for i in range(p...  2.8 us
  transfers between devices with their start and end apart: 12, of which 9 were waited for; matrix products, arithmetic and copies ran while one was open for 4% of the time, Pallas kernels for 12%

profile of v2, /device:TPU:0, one launch (start us, length us, event | category | flops | bytes accessed | tf_op | source)
XLA Modules:
  0.0 73.1 jit_solution(8260046170601457490)
XLA Ops:
  0.6 0.8 %pad_maximum_fusion.1 = f32[80,128]{1,0:T(8,128)S(1)} fusion(f32[8,128]{1,0:T(8,128)} %bitcast.19, f32[8,128]{1,0:T(8,128)} %bitcast.20, f32[64,128]{1,0:T(8,128)} %bitcast.16), kind=kLoop, calls=%fused_computation.1 | loop fusion | flops 20480 | bytes 81920 | tf_op jit(solution)/shard_map/concatenate | solution.py:407
  1.4 5.0 %collective-permute-start.2 = (f32[80,128]{1,0:T(8,128)S(1)}, f32[80,128]{1,0:T(8,128)S(1)}, u32[]{:S(2)}, u32[]{:S(2)}) collective-permute-start(f32[80,128]{1,0:T(8,128)S(1)} %pad_maximum_fusion.1), channel_id=1, source_target_pairs={{0,24},{4,28},{8,0},{12,4},{16,8},{20,12},{24,16},{28,20},{1,25},{... | collective-permute-start | bytes 122888 | tf_op jit(solution)/shard_map/ppermute | solution.py:418
  6.5 0.0 collective-permute-start.1
  6.5 1.0 %collective-permute-start = (f32[80,128]{1,0:T(8,128)S(1)}, f32[80,128]{1,0:T(8,128)S(1)}, u32[]{:S(2)}, u32[]{:S(2)}) collective-permute-start(f32[80,128]{1,0:T(8,128)S(1)} %pad_maximum_fusion.1), channel_id=1, source_target_pairs={{0,8},{4,12},{8,16},{12,20},{16,24},{20,28},{24,0},{28,4},{1,9},{5... | collective-permute-start | bytes 122888 | tf_op jit(solution)/shard_map/ppermute | solution.py:418
  7.5 0.7 pad_bitcast_fusion
  8.1 0.7 pad_bitcast_fusion.1
  8.8 0.8 %pad_maximum_fusion.2.real_ref = f32[64,128]{1,0:T(8,128)S(1)} fusion(f32[1,128]{1,0:T(1,128)S(1)} %pad_bitcast_fusion, f32[7,128]{1,0:T(8,128)} %param.13, f32[56,128]{1,0:T(8,128)} %bitcast.17), kind=kLoop, calls=%fused_computation.2 | loop fusion | flops 16384 | bytes 65536 | tf_op jit(solution)/shard_map/concatenate | solution.py:425
  9.6 0.7 pad_add_fusion.whole_ref
  10.3 0.1 early.1
  10.4 0.0 collective-permute-done.2
  10.4 1.0 %collective-permute-done.1 = f32[80,128]{1,0:T(8,128)S(1)} collective-permute-done((f32[80,128]{1,0:T(8,128)S(1)}, f32[80,128]{1,0:T(8,128)S(1)}, u32[]{:S(2)}, u32[]{:S(2)}) %collective-permute-start.1) | collective-permute-done | bytes 40992 | tf_op jit(solution)/shard_map/ppermute | solution.py:418
  11.4 0.9 %collective-permute-done = f32[80,128]{1,0:T(8,128)S(1)} collective-permute-done((f32[80,128]{1,0:T(8,128)S(1)}, f32[80,128]{1,0:T(8,128)S(1)}, u32[]{:S(2)}, u32[]{:S(2)}) %collective-permute-start) | collective-permute-done | bytes 40992 | tf_op jit(solution)/shard_map/ppermute | solution.py:418
  12.3 1.6 %collective-permute-start.3 = (f32[320,128]{1,0:T(8,128)S(1)}, f32[320,128]{1,0:T(8,128)S(1)}, u32[]{:S(2)}, u32[]{:S(2)}) collective-permute-start(f32[320,128]{1,0:T(8,128)S(1)} %pad_maximum_fusion.near_ref), channel_id=1, source_target_pairs={{0,4},{4,0},{8,12},{12,8},{16,20},{20,16},{24,28},{28,24},{1,5},{5... | collective-permute-start | bytes 491528 | tf_op jit(solution)/shard_map/ppermute | solution.py:27
  13.9 3.8 %collective-permute-done.3.far_ref = f32[320,128]{1,0:T(8,128)S(1)} collective-permute-done((f32[320,128]{1,0:T(8,128)S(1)}, f32[320,128]{1,0:T(8,128)S(1)}, u32[]{:S(2)}, u32[]{:S(2)}) %collective-permute-start.3) | collective-permute-done | bytes 163872 | tf_op jit(solution)/shard_map/ppermute | solution.py:27
  17.7 23.4 %leaf.1 = (f32[768,768]{1,0:T(8,128)S(1)}, f32[408,1024]{1,0:T(8,128)S(1)}, f32[408,128]{1,0:T(8,128)S(1)}, f32[432,128]{1,0:T(8,128)S(1)}) custom-call(s32[8,128]{1,0:T(8,128)S(1)} %get-tuple-element.36.code_ref, s32[8,128]{1,0:T(8,128)S(1)} %get-tuple-element.37.lane_ref, f32[8,128]{1,0:T(8,128)S(1)} %get-tuple-element.38.scale_ref, ...), custom_call_target="tpu_custom_call" | custom-call | tf_op jit(solution)/shard_map/leaf/pallas_call | solution.py:443
  41.0 1.6 %collective-permute-start.4 = (f32[408,128]{1,0:T(8,128)S(1)}, f32[408,128]{1,0:T(8,128)S(1)}, u32[]{:S(2)}, u32[]{:S(2)}) collective-permute-start(f32[408,128]{1,0:T(8,128)S(1)} %get-tuple-element.42.own_ref), channel_id=1, source_target_pairs={{0,4},{4,0},{8,12},{12,8},{16,20},{20,16},{24,28},{28,24},{1,5},{5... | collective-permute-start | bytes 626696 | tf_op jit(solution)/shard_map/ppermute | solution.py:27
  42.6 0.5 collective-permute-start.5
  43.1 2.9 %back.1.solved_ref = f32[408,1024]{1,0:T(8,128)S(1)} custom-call(f32[768,768]{1,0:T(8,128)S(1)} %get-tuple-element.43.lower_ref, f32[408,1024]{1,0:T(8,128)S(1)} %get-tuple-element.44.aug_ref), custom_call_target="tpu_custom_call" | custom-call | flops 2566914048 | tf_op jit(solution)/shard_map/back/pallas_call | solution.py:463
  46.1 1.7 %collective-permute-done.4.other_ref = f32[408,128]{1,0:T(8,128)S(1)} collective-permute-done((f32[408,128]{1,0:T(8,128)S(1)}, f32[408,128]{1,0:T(8,128)S(1)}, u32[]{:S(2)}, u32[]{:S(2)}) %collective-permute-start.4) | collective-permute-done | bytes 208928 | tf_op jit(solution)/shard_map/ppermute | solution.py:27
  47.8 2.0 %height_1.1 = (f32[280,128]{1,0:T(8,128)S(1)}, f32[280,128]{1,0:T(8,128)S(1)}) custom-call(f32[408,128]{1,0:T(8,128)S(1)} %get-tuple-element.42.own_ref, f32[408,128]{1,0:T(8,128)S(1)} %collective-permute-done.4.other_ref), custom_call_target="tpu_custom_call" | custom-call | tf_op jit(solution)/shard_map/height_1/pallas_call | solution.py:478
  49.8 0.4 collective-permute-done.5.other_ref
  50.2 0.5 reduce_1.1
  50.7 1.3 %collective-permute-start.6 = (f32[280,128]{1,0:T(8,128)S(1)}, f32[280,128]{1,0:T(8,128)S(1)}, u32[]{:S(2)}, u32[]{:S(2)}) collective-permute-start(f32[280,128]{1,0:T(8,128)S(1)} %get-tuple-element.49.own_ref), channel_id=1, source_target_pairs={{0,8},{4,12},{8,0},{12,4},{16,24},{20,28},{24,16},{28,20},{1,9},{5... | collective-permute-start | bytes 430088 | tf_op jit(solution)/shard_map/ppermute | solution.py:27
  52.0 0.8 %collective-permute-start.7 = (f32[152,128]{1,0:T(8,128)S(1)}, f32[152,128]{1,0:T(8,128)S(1)}, u32[]{:S(2)}, u32[]{:S(2)}) collective-permute-start(f32[152,128]{1,0:T(8,128)S(1)} %get-tuple-element.54.own_ref), channel_id=1, source_target_pairs={{0,8},{4,12},{8,0},{12,4},{16,24},{20,28},{24,16},{28,20},{1,9},{5... | collective-permute-start | bytes 233480 | tf_op jit(solution)/shard_map/ppermute | solution.py:27
  52.8 1.0 %apply_1.1.solved_ref = f32[280,1024]{1,0:T(8,128)S(1)} custom-call(f32[280,128]{1,0:T(8,128)S(1)} %get-tuple-element.46.coefficient_ref, f32[408,1024]{1,0:T(8,128)S(1)} %back.1.solved_ref), custom_call_target="tpu_custom_call" | custom-call | flops 440401920 | tf_op jit(solution)/shard_map/apply_1/pallas_call | solution.py:499
  53.9 2.0 %collective-permute-done.6.other_ref = f32[280,128]{1,0:T(8,128)S(1)} collective-permute-done((f32[280,128]{1,0:T(8,128)S(1)}, f32[280,128]{1,0:T(8,128)S(1)}, u32[]{:S(2)}, u32[]{:S(2)}) %collective-permute-start.6) | collective-permute-done | bytes 143392 | tf_op jit(solution)/shard_map/ppermute | solution.py:27
  55.9 1.9 %height_2.1 = (f32[152,128]{1,0:T(8,128)S(1)}, f32[152,128]{1,0:T(8,128)S(1)}) custom-call(f32[280,128]{1,0:T(8,128)S(1)} %get-tuple-element.49.own_ref, f32[280,128]{1,0:T(8,128)S(1)} %collective-permute-done.6.other_ref), custom_call_target="tpu_custom_call" | custom-call | tf_op jit(solution)/shard_map/height_2/pallas_call | solution.py:478
  57.7 0.0 collective-permute-done.7.other_ref
  57.8 0.3 reduce_2.1.own_ref
  58.1 1.6 %collective-permute-start.8 = (f32[152,128]{1,0:T(8,128)S(1)}, f32[152,128]{1,0:T(8,128)S(1)}, u32[]{:S(2)}, u32[]{:S(2)}) collective-permute-start(f32[152,128]{1,0:T(8,128)S(1)} %reduce_2.1.own_ref), channel_id=1, source_target_pairs={{0,16},{4,20},{8,24},{12,28},{16,0},{20,4},{24,8},{28,12},{1,17},{... | collective-permute-start | bytes 233480 | tf_op jit(solution)/shard_map/ppermute | solution.py:27
  59.7 0.7 apply_2.1.solved_ref
  60.4 3.9 %collective-permute-done.8.other_ref = f32[152,128]{1,0:T(8,128)S(1)} collective-permute-done((f32[152,128]{1,0:T(8,128)S(1)}, f32[152,128]{1,0:T(8,128)S(1)}, u32[]{:S(2)}, u32[]{:S(2)}) %collective-permute-start.8) | collective-permute-done | bytes 77856 | tf_op jit(solution)/shard_map/ppermute | solution.py:27
  64.2 3.0 %final.1 = (f32[1,1024]{1,0:T(1,128)}, f32[16,1024]{1,0:T(8,128)}, f32[1,1024]{1,0:T(1,128)S(1)}) custom-call(f32[152,128]{1,0:T(8,128)S(1)} %reduce_2.1.own_ref, f32[152,128]{1,0:T(8,128)S(1)} %collective-permute-done.8.other_ref, f32[152,1024]{1,0:T(8,128)S(1)} %apply_2.1.solved_ref, f32[16,1024]{1,0:T(8,128)S(1)} %get-tuple-element.40.sign_ref), custom_call_target="tpu_custom_call" | custom-call | tf_op jit(solution)/shard_map/final/pallas_call | solution.py:509
  67.2 0.0 collective-permute-start.11
  67.3 1.5 %collective-permute-start.10 = (f32[1,1024]{1,0:T(1,128)S(1)}, f32[1,1024]{1,0:T(1,128)S(1)}, u32[]{:S(2)}, u32[]{:S(2)}) collective-permute-start(f32[1,1024]{1,0:T(1,128)S(1)} %get-tuple-element.58), channel_id=1, source_target_pairs={{0,2},{1,3},{2,0},{3,1},{4,6},{5,7},{6,4},{7,5},{8,10},{9,11},{10,... | collective-permute-start | bytes 12296 | tf_op jit(solution)/shard_map/ppermute | solution.py:524
  68.8 0.2 collective-permute-start.9
  69.0 0.0 collective-permute-done.11
  69.0 1.9 %collective-permute-done.10 = f32[1,1024]{1,0:T(1,128)S(1)} collective-permute-done((f32[1,1024]{1,0:T(1,128)S(1)}, f32[1,1024]{1,0:T(1,128)S(1)}, u32[]{:S(2)}, u32[]{:S(2)}) %collective-permute-start.10) | collective-permute-done | bytes 4128 | tf_op jit(solution)/shard_map/ppermute | solution.py:524
  70.9 0.9 %collective-permute-done.9 = f32[1,1024]{1,0:T(1,128)S(1)} collective-permute-done((f32[1,1024]{1,0:T(1,128)S(1)}, f32[1,1024]{1,0:T(1,128)S(1)}, u32[]{:S(2)}, u32[]{:S(2)}) %collective-permute-start.9) | collective-permute-done | bytes 4128 | tf_op jit(solution)/shard_map/ppermute | solution.py:524
  71.8 1.3 %fusion = f32[1024]{0:T(1024)} fusion(f32[1024]{0:T(1024)S(1)} %bitcast.18, f32[1024]{0:T(1024)} %bitcast.22), kind=kLoop, calls=%fused_computation.5 | loop fusion | flops 3072 | bytes 12288 | tf_op jit(solution)/shard_map/sub | solution.py:528
  (2 shorter events, 0.0 us)
Async XLA Ops:
  1.4 9.0 %collective-permute-start.2 = (f32[80,128]{1,0:T(8,128)S(1)}, f32[80,128]{1,0:T(8,128)S(1)}, u32[]{:S(2)}, u32[]{:S(2)}) collective-permute-start(f32[80,128]{1,0:T(8,128)S(1)} %pad_maximum_fusion.1), channel_id=1, source_target_pairs={{0,24},{4,28},{8,0},{12,4},{16,8},{20,12},{24,16},{28,20},{1,25},{... | collective-permute-start | bytes 122888 | tf_op jit(solution)/shard_map/ppermute | solution.py:418
  6.5 4.9 %collective-permute-start.1 = (f32[80,128]{1,0:T(8,128)S(1)}, f32[80,128]{1,0:T(8,128)S(1)}, u32[]{:S(2)}, u32[]{:S(2)}) collective-permute-start(f32[80,128]{1,0:T(8,128)S(1)} %pad_maximum_fusion.1), channel_id=1, source_target_pairs={{0,16},{4,20},{8,24},{12,28},{16,0},{20,4},{24,8},{28,12},{1,17},{... | collective-permute-start | bytes 122888 | tf_op jit(solution)/shard_map/ppermute | solution.py:418
  6.5 5.8 %collective-permute-start = (f32[80,128]{1,0:T(8,128)S(1)}, f32[80,128]{1,0:T(8,128)S(1)}, u32[]{:S(2)}, u32[]{:S(2)}) collective-permute-start(f32[80,128]{1,0:T(8,128)S(1)} %pad_maximum_fusion.1), channel_id=1, source_target_pairs={{0,8},{4,12},{8,16},{12,20},{16,24},{20,28},{24,0},{28,4},{1,9},{5... | collective-permute-start | bytes 122888 | tf_op jit(solution)/shard_map/ppermute | solution.py:418
  12.3 5.4 %collective-permute-start.3 = (f32[320,128]{1,0:T(8,128)S(1)}, f32[320,128]{1,0:T(8,128)S(1)}, u32[]{:S(2)}, u32[]{:S(2)}) collective-permute-start(f32[320,128]{1,0:T(8,128)S(1)} %pad_maximum_fusion.near_ref), channel_id=1, source_target_pairs={{0,4},{4,0},{8,12},{12,8},{16,20},{20,16},{24,28},{28,24},{1,5},{5... | collective-permute-start | bytes 491528 | tf_op jit(solution)/shard_map/ppermute | solution.py:27
  41.0 6.8 %collective-permute-start.4 = (f32[408,128]{1,0:T(8,128)S(1)}, f32[408,128]{1,0:T(8,128)S(1)}, u32[]{:S(2)}, u32[]{:S(2)}) collective-permute-start(f32[408,128]{1,0:T(8,128)S(1)} %get-tuple-element.42.own_ref), channel_id=1, source_target_pairs={{0,4},{4,0},{8,12},{12,8},{16,20},{20,16},{24,28},{28,24},{1,5},{5... | collective-permute-start | bytes 626696 | tf_op jit(solution)/shard_map/ppermute | solution.py:27
  42.6 7.6 %collective-permute-start.5 = (f32[432,128]{1,0:T(8,128)S(1)}, f32[432,128]{1,0:T(8,128)S(1)}, u32[]{:S(2)}, u32[]{:S(2)}) collective-permute-start(f32[432,128]{1,0:T(8,128)S(1)} %get-tuple-element.48.own_ref), channel_id=1, source_target_pairs={{0,4},{4,0},{8,12},{12,8},{16,20},{20,16},{24,28},{28,24},{1,5},{5... | collective-permute-start | bytes 663560 | tf_op jit(solution)/shard_map/ppermute | solution.py:27
  50.7 5.2 %collective-permute-start.6 = (f32[280,128]{1,0:T(8,128)S(1)}, f32[280,128]{1,0:T(8,128)S(1)}, u32[]{:S(2)}, u32[]{:S(2)}) collective-permute-start(f32[280,128]{1,0:T(8,128)S(1)} %get-tuple-element.49.own_ref), channel_id=1, source_target_pairs={{0,8},{4,12},{8,0},{12,4},{16,24},{20,28},{24,16},{28,20},{1,9},{5... | collective-permute-start | bytes 430088 | tf_op jit(solution)/shard_map/ppermute | solution.py:27
  52.0 5.8 %collective-permute-start.7 = (f32[152,128]{1,0:T(8,128)S(1)}, f32[152,128]{1,0:T(8,128)S(1)}, u32[]{:S(2)}, u32[]{:S(2)}) collective-permute-start(f32[152,128]{1,0:T(8,128)S(1)} %get-tuple-element.54.own_ref), channel_id=1, source_target_pairs={{0,8},{4,12},{8,0},{12,4},{16,24},{20,28},{24,16},{28,20},{1,9},{5... | collective-permute-start | bytes 233480 | tf_op jit(solution)/shard_map/ppermute | solution.py:27
  58.1 6.2 %collective-permute-start.8 = (f32[152,128]{1,0:T(8,128)S(1)}, f32[152,128]{1,0:T(8,128)S(1)}, u32[]{:S(2)}, u32[]{:S(2)}) collective-permute-start(f32[152,128]{1,0:T(8,128)S(1)} %reduce_2.1.own_ref), channel_id=1, source_target_pairs={{0,16},{4,20},{8,24},{12,28},{16,0},{20,4},{24,8},{28,12},{1,17},{... | collective-permute-start | bytes 233480 | tf_op jit(solution)/shard_map/ppermute | solution.py:27
  67.2 1.7 %collective-permute-start.11 = (f32[1,1024]{1,0:T(1,128)S(1)}, f32[1,1024]{1,0:T(1,128)S(1)}, u32[]{:S(2)}, u32[]{:S(2)}) collective-permute-start(f32[1,1024]{1,0:T(1,128)S(1)} %get-tuple-element.58), channel_id=1, source_target_pairs={{0,3},{1,0},{2,1},{3,2},{4,7},{5,4},{6,5},{7,6},{8,11},{9,8},{10,9... | collective-permute-start | bytes 12296 | tf_op jit(solution)/shard_map/ppermute | solution.py:524
  67.3 3.6 %collective-permute-start.10 = (f32[1,1024]{1,0:T(1,128)S(1)}, f32[1,1024]{1,0:T(1,128)S(1)}, u32[]{:S(2)}, u32[]{:S(2)}) collective-permute-start(f32[1,1024]{1,0:T(1,128)S(1)} %get-tuple-element.58), channel_id=1, source_target_pairs={{0,2},{1,3},{2,0},{3,1},{4,6},{5,7},{6,4},{7,5},{8,10},{9,11},{10,... | collective-permute-start | bytes 12296 | tf_op jit(solution)/shard_map/ppermute | solution.py:524
  68.8 3.0 %collective-permute-start.9 = (f32[1,1024]{1,0:T(1,128)S(1)}, f32[1,1024]{1,0:T(1,128)S(1)}, u32[]{:S(2)}, u32[]{:S(2)}) collective-permute-start(f32[1,1024]{1,0:T(1,128)S(1)} %get-tuple-element.58), channel_id=1, source_target_pairs={{0,1},{1,2},{2,3},{3,0},{4,5},{5,6},{6,7},{7,4},{8,9},{9,10},{10,1... | collective-permute-start | bytes 12296 | tf_op jit(solution)/shard_map/ppermute | solution.py:524
